TPU v7x, 256 devices: a whole 4x4x8 slice. The times are simulated.
256 devices in a mesh: species: 8 (over x, y_hi), ctx: 32 (over y_lo, z, core).
Axes of the slice: x: 4, y: 4 (y_hi: 2, y_lo: 2; y = y_hi * 2 + y_lo), z: 8, core: 2. Of those that a mesh axis runs over, the one named last changes fastest.
Arguments:
- tokens: bfloat16 [8, 16384, 1024], P('species', 'ctx'), may hold values from -6 to 6
- gap_mask: int32 [8, 32], replicated, may hold values from 0 to 1, as said below
- window_reach: int32 [32], replicated, may hold values from 128 to 512
- row_qkv: bfloat16 [1024, 1536], replicated
- row_out: bfloat16 [512, 1024], replicated, may hold values from -3 to 3
- col_qkv: bfloat16 [1024, 1536], replicated
- col_out: bfloat16 [512, 1024], replicated, may hold values from -0.5 to 0.5
Outputs:
- mixed: bfloat16 [8, 16384, 1024], P('species', 'ctx')
Inputs may be any that keep to these rules, and one draw needn't show every extreme that they name: `gap_mask`: species row 0 is 1 in every block.
All inputs are finite; a program needn't handle non-finite values.
Results may differ from a plain program's by a relative error of at most 0.015.
Values may be sent and summed in bfloat16 or wider, within the bound.
No kernel may reach another device: no remote copies, remote signals or barrier semaphores. Data moves between devices by JAX's collectives and lax.ppermute only.
A program may use at most 128 MiB of HBM per device.

v0:
```python
import jax
import jax.numpy as jnp
from jax import lax
from jax.sharding import PartitionSpec as P

HEAD = 64


def with_halo(cells, sides, width):
    for axis, dim in sides:
        count = lax.axis_size(axis)
        head = lax.slice_in_dim(cells, 0, width, axis=dim)
        tail = lax.slice_in_dim(cells, cells.shape[dim] - width, cells.shape[dim], axis=dim)
        cells = jnp.concatenate(
            [
                lax.ppermute(tail, axis, [(i, (i + 1) % count) for i in range(count)]),
                cells,
                lax.ppermute(head, axis, [((i + 1) % count, i) for i in range(count)]),
            ],
            axis=dim,
        )
    return cells


def rms_rows(values):
    return values * lax.rsqrt(jnp.mean(values * values, axis=-1, keepdims=True) + 1e-06)


def softmax_last(scores):
    maxima = jnp.max(scores, axis=-1, keepdims=True)
    expsum = jnp.exp(scores - maxima)
    return expsum / jnp.sum(expsum, axis=-1, keepdims=True)


def row_attend(queries, keyval, usable):
    blocklen = queries.shape[0]
    keylen = keyval.shape[0]
    half_width = queries.shape[1]
    head_count = half_width // HEAD
    query_heads = queries.reshape(blocklen, head_count, HEAD)
    key_heads = keyval[:, :half_width].reshape(keylen, head_count, HEAD)
    value_heads = keyval[:, half_width:].reshape(keylen, head_count, HEAD)
    scores = jnp.einsum(
        "qhd,khd->hqk", query_heads, key_heads, preferred_element_type=jnp.float32
    ) * HEAD ** (-0.5)
    scores = jnp.where(usable[None, None, :], scores, -1e30)
    weights = softmax_last(scores).astype(jnp.bfloat16)
    attended = jnp.einsum("hqk,khd->qhd", weights, value_heads, preferred_element_type=jnp.float32)
    return attended.astype(jnp.bfloat16).reshape(blocklen, half_width)


def column_attend(queries, keyval, alive):
    query_count, columns, half_width = queries.shape
    key_count = keyval.shape[0]
    head_count = half_width // HEAD
    query_heads = queries.reshape(query_count, columns, head_count, HEAD)
    key_heads = keyval[..., :half_width].reshape(key_count, columns, head_count, HEAD)
    value_heads = keyval[..., half_width:].reshape(key_count, columns, head_count, HEAD)
    scores = jnp.einsum(
        "schd,tchd->hsct", query_heads, key_heads, preferred_element_type=jnp.float32
    ) * HEAD ** (-0.5)
    scores = jnp.where(alive[None, None, None, :], scores, -1e30)
    weights = softmax_last(scores).astype(jnp.bfloat16)
    attended = jnp.einsum(
        "hsct,tchd->schd", weights, value_heads, preferred_element_type=jnp.float32
    )
    return attended.astype(jnp.bfloat16).reshape(query_count, columns, half_width)


def body(tokens, gap_mask, window_reach, row_qkv, row_out, col_qkv, col_out):
    local_species, blocklen, features = tokens.shape
    half_width = row_out.shape[0]
    block_id = lax.axis_index("ctx")
    block_count = lax.axis_size("ctx")
    species_id = lax.axis_index("species")
    normed = rms_rows(tokens.astype(jnp.float32)).astype(jnp.bfloat16)
    packed = jnp.dot(
        normed.reshape(-1, features), row_qkv, preferred_element_type=jnp.float32
    ).astype(jnp.bfloat16)
    packed = packed.reshape(local_species, blocklen, 3 * half_width)
    keyval_wide = with_halo(packed[..., half_width:], (("ctx", 1),), blocklen)
    before_blk = (block_id + block_count - 1) % block_count
    after_blk = (block_id + 1) % block_count
    gaps_mine = lax.dynamic_slice_in_dim(gap_mask, species_id * local_species, local_species, 0)
    before_ok = lax.dynamic_index_in_dim(gaps_mine, before_blk, 1, keepdims=False) == 1
    after_ok = lax.dynamic_index_in_dim(gaps_mine, after_blk, 1, keepdims=False) == 1
    reach_now = lax.dynamic_index_in_dim(window_reach, block_id, 0, keepdims=False)
    offsets = jnp.arange(3 * blocklen, dtype=jnp.int32)
    in_before = (offsets < blocklen) & (offsets >= blocklen - reach_now)
    in_middle = (offsets >= blocklen) & (offsets < 2 * blocklen)
    in_after = (offsets >= 2 * blocklen) & (offsets < 2 * blocklen + reach_now)
    usable = (
        in_middle[None, :]
        | in_before[None, :] & before_ok[:, None]
        | in_after[None, :] & after_ok[:, None]
    )
    attended = lax.map(
        lambda item: row_attend(item[0], item[1], item[2]),
        (packed[..., :half_width], keyval_wide, usable),
    )
    middle = tokens.astype(jnp.float32) + jnp.dot(
        attended.reshape(-1, half_width), row_out, preferred_element_type=jnp.float32
    ).reshape(local_species, blocklen, features)
    col_normed = rms_rows(middle).astype(jnp.bfloat16)
    alive = lax.dynamic_index_in_dim(gap_mask, block_id, 1, keepdims=False) == 1
    col_packed = jnp.dot(
        col_normed.reshape(-1, features), col_qkv, preferred_element_type=jnp.float32
    ).astype(jnp.bfloat16)
    col_packed = col_packed.reshape(local_species, blocklen, 3 * half_width)
    keyval_all = lax.all_gather(col_packed[..., half_width:], "species", axis=0, tiled=True)
    col_attended = column_attend(col_packed[..., :half_width], keyval_all, alive)
    result = middle + jnp.dot(
        col_attended.reshape(-1, half_width), col_out, preferred_element_type=jnp.float32
    ).reshape(local_species, blocklen, features)
    return result.astype(jnp.bfloat16)


def solution(mesh):
    placed = (P("species", "ctx", None), P(), P(), P(), P(), P(), P())
    return jax.shard_map(
        body, mesh=mesh, in_specs=placed, out_specs=P("species", "ctx", None), check_vma=False
    )
```

profile of v0, /device:TPU:96, one launch (start us, length us, event | category | flops | bytes accessed | tf_op | source)
XLA Modules:
  0.0 217.5 jit_solution(2765976548111695860)
XLA Ops:
  6.5 1.7 fusion.10
  8.2 0.5 copy-done
  8.7 3.1 %fusion.8 = bf16[1,512,1536]{2,1,0:T(8,128)(2,1)S(1)} fusion(bf16[1024,1536]{1,0:T(8,128)(2,1)S(1)} %copy-done, bf16[1,512,1024]{2,1,0:T(8,128)(2,1)} %param.7, f32[512]{0:T(512)S(1)} %add_rsqrt_fusion.1), kind=kOutput, calls=%fused_computation.19 | convolution fusion | flops 1612972032 | bytes 5769216 | tf_op jit(solution)/shard_map/dot_general | solution.py:77
  11.8 1.1 copy-done.3
  13.0 1.1 slice.34
  14.1 0.5 collective-permute-start
  14.6 1.9 slice.36
  16.5 0.7 fusion.55
  18.4 0.6 dynamic_slice.25
  20.1 2.1 copy.24
  22.2 4.5 %collective-permute-done.1 = bf16[1,512,1024]{2,1,0:T(8,128)(2,1)} collective-permute-done((bf16[1,512,1024]{2,1,0:T(8,128)(2,1)}, bf16[1,512,1024]{2,1,0:T(8,128)(2,1)}, u32[]{:S(2)}, u32[]{:S(2)}) %collective-permute-start.1) | collective-permute-done | bytes 1048608 | tf_op jit(solution)/shard_map/ppermute | solution.py:18
  26.7 1.9 collective-permute-done
  28.6 2.0 maximum_bitcast_fusion
  30.7 1.9 fusion.54
  32.5 2.6 %copy.25 = bf16[1536,512]{0,1:T(8,128)(2,1)} copy(bf16[1536,512]{1,0:T(8,128)(2,1)} %get-tuple-element.20) | data formatting | bytes 3145728 | tf_op jit(solution)/shard_map/while/body/eval_jaxpr/slice | solution.py:41
  35.1 2.6 %copy.23 = bf16[1536,512]{0,1:T(8,128)(2,1)} copy(bf16[1536,512]{1,0:T(8,128)(2,1)} %get-tuple-element.22) | data formatting | bytes 3145728 | tf_op jit(solution)/shard_map/while/body/eval_jaxpr/slice | solution.py:42
  37.7 8.8 %fusion.56 = f32[8,512]{1,0:T(8,128)S(1)} fusion(pred[1536]{0:T(1024)(128)(4,1)S(1)} %fusion.37, bf16[512,8,64]{0,2,1:T(8,128)(2,1)} %bitcast.62, bf16[1536,8,64]{0,2,1:T(8,128)(2,1)} %bitcast.58), kind=kOutput, calls=%fused_computation.72 | convolution fusion | flops 830473728 | bytes 2115072 | tf_op jit(solution)/shard_map/while/body/eval_jaxpr/sub | solution.py:31
  46.5 11.8 %fusion.13 = bf16[8,64,512]{2,1,0:T(8,128)(2,1)} fusion(bf16[1536,8,64]{0,2,1:T(8,128)(2,1)} %bitcast.60, f32[8,512]{1,0:T(8,128)S(1)} %fusion.56, pred[1536]{0:T(1024)(128)(4,1)S(1)} %fusion.37, bf16[512,8,64]{0,2,1:T(8,128)(2,1)} %bitcast.63, bf16[1536,8,64]{0,2,1:T(8,128)(2,1)} %bitcast.59), kind=kOutput, calls=%fused_computation.27 | convolution fusion | flops 1642337792 | bytes 4212224 | tf_op jit(solution)/shard_map/while/body/eval_jaxpr/hqk,khd->qhd/dot_general | solution.py:48
  58.3 2.7 %multiply_reduce_fusion.2 = (f32[512]{0:T(512)S(1)}, f32[1,512,1024]{2,1,0:T(8,128)S(1)}) fusion(bf16[512,512]{0,1:T(8,128)(2,1)} %bitcast.61, bf16[512,1024]{1,0:T(8,128)(2,1)} %param.11, bf16[1,512,1024]{2,1,0:T(8,128)(2,1)} %param.7), kind=kOutput, calls=%fused_computation.26 | convolution fusion | flops 538967552 | bytes 4720640 | tf_op jit(solution)/shard_map/dot_general | solution.py:101
  61.0 1.9 fusion.9
  62.9 1.2 copy-done.4
  64.1 1.1 slice.38
  65.5 1.9 slice.41
  67.3 2.1 copy.44
  69.4 2.2 convert.1
  71.6 111.2 %all-gather.2.cloned.1.call-done = bf16[8,512,1024]{2,1,0:T(8,128)(2,1)} async-done(((bf16[1,512,1024]{2,1,0:T(8,128)(2,1)}), bf16[8,512,1024]{2,1,0:T(8,128)(2,1)}) %all-gather.2.cloned.1.call-update) | async-done | bytes 8388624 | tf_op jit(solution)/shard_map/all_gather | solution.py:110
  182.8 5.7 %fusion.53 = (bf16[8,512,512]{2,1,0:T(8,128)(2,1)}, bf16[8,512,512]{2,1,0:T(8,128)(2,1)}) fusion(bf16[8,512,1024]{2,1,0:T(8,128)(2,1)} %all-gather.2.cloned.1.call-done), kind=kLoop, calls=%fused_computation.69 | loop fusion | bytes 16777216 | tf_op jit(solution)/shard_map/slice | solution.py:57
  188.6 6.5 %copy.46 = bf16[8,512,512]{1,2,0:T(8,128)(2,1)} copy(bf16[8,512,512]{2,1,0:T(8,128)(2,1)} %get-tuple-element.13) | data formatting | bytes 8388608
  195.0 3.9 %multiply_reduce_fusion.1 = f32[8,512,8]{1,0,2:T(8,128)S(1)} fusion(f32[8,512,64]{1,2,0:T(8,128)} %convert.1, bf16[8,512,512]{1,2,0:T(8,128)(2,1)} %copy.46), kind=kLoop, calls=%fused_computation.12 | loop fusion | flops 6258688 | bytes 5373952
  199.1 6.5 %copy.45 = bf16[8,512,512]{1,2,0:T(8,128)(2,1)} copy(bf16[8,512,512]{2,1,0:T(8,128)(2,1)} %get-tuple-element.14) | data formatting | bytes 8388608
  205.6 3.3 %multiply_reduce_fusion = bf16[512,8,64]{0,2,1:T(8,128)(2,1)S(1)} fusion(bf16[512,8,8,64]{0,3,1,2:T(8,128)(2,1)} %bitcast.55, f32[512,8,8]{0,1,2:T(8,128)S(1)} %copy.48), kind=kLoop, calls=%fused_computation.11 | loop fusion | flops 6029312 | bytes 4849664 | tf_op jit(solution)/shard_map/hsct,tchd->schd/dot_general | solution.py:64
  208.9 1.7 fusion.12
  (24 shorter events, 0.5 us)
Async XLA Ops:
  6.5 2.2 %copy-start = (bf16[1024,1536]{1,0:T(8,128)(2,1)S(1)}, bf16[1024,1536]{1,0:T(8,128)(2,1)}, u32[]{:S(2)}) copy-start(bf16[1024,1536]{1,0:T(8,128)(2,1)} %param.10) | copy-start | bytes 9437188
  6.5 176.3 %all-gather.2.cloned.1.call-start = ((), (), s32[]{:S(2)}) async-start(), calls=%async_computation | async-start | bytes 9437184 | tf_op jit(solution)/shard_map/all_gather | solution.py:110
  11.8 1.2 copy-start.3
  13.0 3.5 %copy-start.6 = (s32[8,32]{1,0:T(8,128)S(1)}, s32[8,32]{1,0:T(8,128)}, u32[]{:S(2)}) copy-start(s32[8,32]{1,0:T(8,128)} %param.8) | copy-start | bytes 3076
  13.0 5.5 %copy-start.8 = (s32[32]{0:T(128)S(1)}, s32[32]{0:T(128)}, u32[]{:S(2)}) copy-start(s32[32]{0:T(128)} %param.9) | copy-start | bytes 388
  14.1 12.6 %collective-permute-start.1 = (bf16[1,512,1024]{2,1,0:T(8,128)(2,1)}, bf16[1,512,1024]{2,1,0:T(8,128)(2,1)}, u32[]{:S(2)}, u32[]{:S(2)}) collective-permute-start(bf16[1,512,1024]{2,1,0:T(8,128)(2,1)} %slice.34), channel_id=1, source_target_pairs={{1,0},{2,1},{3,2},{4,3},{5,4},{6,5},{7,6},{8,7},{9,8},{10,9},{11,1... | collective-permute-start | bytes 3145736 | tf_op jit(solution)/shard_map/ppermute | solution.py:18
  14.1 14.5 %collective-permute-start = (bf16[1,512,1024]{2,1,0:T(8,128)(2,1)}, bf16[1,512,1024]{2,1,0:T(8,128)(2,1)}, u32[]{:S(2)}, u32[]{:S(2)}) collective-permute-start(bf16[1,512,1024]{2,1,0:T(8,128)(2,1)} %slice.34), channel_id=1, source_target_pairs={{0,1},{1,2},{2,3},{3,4},{4,5},{5,6},{6,7},{7,8},{8,9},{9,10},{10,1... | collective-permute-start | bytes 3145736 | tf_op jit(solution)/shard_map/ppermute | solution.py:16
  58.3 2.7 %copy-start.7 = (bf16[1024,1536]{1,0:T(8,128)(2,1)S(1)}, bf16[1024,1536]{1,0:T(8,128)(2,1)}, u32[]{:S(2)}) copy-start(bf16[1024,1536]{1,0:T(8,128)(2,1)} %param.12) | copy-start | bytes 9437188
  61.0 1.9 copy-start.1
  62.9 1.2 copy-start.4
  205.6 3.3 %copy-start.2 = (f32[1,512,1024]{2,1,0:T(8,128)S(1)}, f32[1,512,1024]{2,1,0:T(8,128)}, u32[]{:S(2)}) copy-start(f32[1,512,1024]{2,1,0:T(8,128)} %copy-done.1) | copy-start | bytes 6291460
  205.6 3.3 %copy-start.5 = (bf16[512,1024]{1,0:T(8,128)(2,1)S(1)}, bf16[512,1024]{1,0:T(8,128)(2,1)}, u32[]{:S(2)}) copy-start(bf16[512,1024]{1,0:T(8,128)(2,1)} %param.13) | copy-start | bytes 3145732
Sparse Core Ops, SparseCore 0:
  65.4 117.3 all-gather.1
where the time goes:
time: 220 us; the launch traced here: 218 us
  waiting for transfers between devices  118 us (54%)
  local copies, waits for them, and re-layouts  40.1 us (18%)
  matrix products  29.9 us (14%)
  between operations  15.9 us (7%)
  other arithmetic  13.4 us (6%)
    all_gather x1, waiting for transfers between devices, body(): lax.all_gather(col_packed[..., half_width:], 'species', axis=0, tiled=True)  111 us
    unnamed x22, local copies, waits for them, and re-layouts  18 us
    dot_general x1, matrix products, row_attend(): jnp.einsum('hqk,khd->qhd', weights, value_heads, preferred_element_type=j...  11.8 us
    sub x1, matrix products, softmax_last(): expsum = jnp.exp(scores - maxima)  8.78 us
    unnamed x2, other arithmetic  6.03 us
    slice x1, local copies, waits for them, and re-layouts, column_attend(): keyval[..., :half_width].reshape(key_count, columns, head_count, HEAD)  5.74 us
    ppermute x1, waiting for transfers between devices, with_halo(): lax.ppermute(head, axis, [((i + 1) % count, i) for i in range(count)])  4.5 us
    slice x2, local copies, waits for them, and re-layouts, row_attend(): key_heads = keyval[:, :half_width].reshape(keylen, head_count, HEAD)  4.45 us
  transfers between devices with their start and end apart: 3, of which 3 were waited for; matrix products, arithmetic and copies ran while one was open for 5% of the time, Pallas kernels for 0%

commit v1 on v0

v1 whole, which is shorter than its diff:
```python
import math

import jax
import jax.numpy as jnp
from jax import lax
from jax.experimental import pallas as pl
from jax.experimental.pallas import tpu as pltpu
from jax.sharding import PartitionSpec as P

HEAD = 64
PAIR = 2 * HEAD
SCALE = HEAD ** (-0.5) / math.log(2.0)
BF = jnp.bfloat16
F32 = jnp.float32
VMEM = pl.BlockSpec(memory_space=pltpu.VMEM)
SMEM = pl.BlockSpec(memory_space=pltpu.SMEM)


def dot(a, b):
    return jnp.dot(a, b, preferred_element_type=F32)


def dot_t(a, b):
    return lax.dot_general(a, b, (((1,), (1,)), ((), ())), preferred_element_type=F32)


def rms(values):
    return values * lax.rsqrt(jnp.mean(values * values, axis=-1, keepdims=True) + 1e-06)


def lower_half(rows):
    return lax.broadcasted_iota(jnp.int32, (rows, PAIR), 1) < HEAD


def one_head(pair, head):
    low = lower_half(pair.shape[0])
    keep = low if head == 0 else ~low
    return jnp.where(keep, pair, jnp.zeros_like(pair))


def values_and_ones(pair, head):
    return jnp.concatenate([one_head(pair, head), one_head(jnp.ones_like(pair), head)], axis=1)


def spread(first, second, rows):
    return jnp.where(
        lower_half(rows),
        jnp.broadcast_to(first, (rows, PAIR)),
        jnp.broadcast_to(second, (rows, PAIR)),
    )


def keyval_kernel(x_ref, w_ref, n_ref, kv0_ref, kv1_ref):
    step = pl.program_id(0)

    @pl.when(step == 0)
    def _():
        n_ref[...] = rms(x_ref[...].astype(F32)).astype(BF)

    out = dot(n_ref[...], w_ref[...]).astype(BF)
    for half in range(2):
        part = out[:, half * PAIR : (half + 1) * PAIR]

        @pl.when(step < 2)
        def _():
            kv0_ref[half] = part

        @pl.when(step >= 2)
        def _():
            kv1_ref[half] = part


def keyval(x, weights):
    rows, features = x.shape
    hd = weights.shape[1] // 3
    grp = hd // 2
    pairs = grp // PAIR
    out = jax.ShapeDtypeStruct((2 * pairs, rows, PAIR), BF)
    return pl.pallas_call(
        keyval_kernel,
        grid=(4,),
        in_specs=[
            pl.BlockSpec((rows, features), lambda j: (0, 0)),
            pl.BlockSpec((features, grp), lambda j: (0, 2 + (j % 2) * 2 + j // 2)),
        ],
        out_specs=[
            pl.BlockSpec((rows, features), lambda j: (0, 0)),
            pl.BlockSpec((pairs, rows, PAIR), lambda j: (jnp.minimum(j, 1), 0, 0)),
            pl.BlockSpec((pairs, rows, PAIR), lambda j: (jnp.maximum(j - 2, 0), 0, 0)),
        ],
        out_shape=[jax.ShapeDtypeStruct((rows, features), BF), out, out],
        compiler_params=pltpu.CompilerParams(vmem_limit_bytes=20 * 2**20),
        name="keyval",
    )(x, weights)


def query_kernel(n_ref, w_ref, q_ref):
    for grp in range(2):
        cols = pl.ds(grp * 2 * PAIR, 2 * PAIR)
        out = (dot(n_ref[...], w_ref[:, cols]) * SCALE).astype(BF)
        q_ref[2 * grp] = out[:, :PAIR]
        q_ref[2 * grp + 1] = out[:, PAIR:]


def queries(normed, weights):
    rows, features = normed.shape
    hd = weights.shape[1] // 3
    return pl.pallas_call(
        query_kernel,
        grid=(1,),
        in_specs=[
            pl.BlockSpec((rows, features), lambda j: (0, 0)),
            pl.BlockSpec((features, hd), lambda j: (0, 0)),
        ],
        out_specs=pl.BlockSpec((hd // PAIR, rows, PAIR), lambda j: (0, 0, 0)),
        out_shape=jax.ShapeDtypeStruct((hd // PAIR, rows, PAIR), BF),
        compiler_params=pltpu.CompilerParams(vmem_limit_bytes=20 * 2**20),
        name="queries",
    )(normed, weights)


def window_of(gap_ref, reach_ref, blocklen, blocks, fast):
    block = lax.axis_index("ctx")
    species = lax.axis_index("species")
    odd = lax.rem(block, 2)
    before = odd == 1 if fast else odd == 0
    other = jnp.where(before, lax.rem(block + blocks - 1, blocks), lax.rem(block + 1, blocks))
    reach = reach_ref[block]
    low = jnp.where(before, blocklen - reach, 0)
    high = jnp.where(before, blocklen, reach)
    high = jnp.where(gap_ref[species, other] == 1, high, 0)
    cols = lax.broadcasted_iota(jnp.int32, (1, blocklen), 1)
    return (cols >= low) & (cols < high)


ROWS = 256


def near_kernel(blocks, gap_ref, reach_ref, q_ref, o0, o1, f0, f1, acc_ref, max_ref):
    rows = q_ref.shape[1]
    seen = window_of(gap_ref, reach_ref, rows, blocks, True)
    for grp, (own, fast) in enumerate(((o0, f0), (o1, f1))):

        def pair_step(i, carry):
            p = 2 * grp + i
            keys_own, keys_fast = own[i], fast[i]
            vals = (own[2 + i], fast[2 + i])
            va = jnp.concatenate([values_and_ones(v, h) for h in range(2) for v in vals], axis=0)
            for t in range(rows // ROWS):
                part = pl.ds(t * ROWS, ROWS)
                q = q_ref[p, part]
                tops, probs = [], []
                for h in range(2):
                    qh = one_head(q, h)
                    so = dot_t(qh, keys_own)
                    sf = jnp.where(seen, dot_t(qh, keys_fast), -1e30)
                    top = jnp.maximum(
                        jnp.max(so, axis=-1, keepdims=True), jnp.max(sf, axis=-1, keepdims=True)
                    )
                    tops.append(top)
                    probs += [jnp.exp2(so - top).astype(BF), jnp.exp2(sf - top).astype(BF)]
                acc_ref[p, part] = dot(jnp.concatenate(probs, axis=1), va)
                max_ref[p, part] = spread(tops[0], tops[1], ROWS)
            return carry

        lax.fori_loop(0, 2, pair_step, 0)


def near_attend(gap_mask, reach, q, own, fast):
    pairs, rows, _ = q.shape
    blocks = gap_mask.shape[1]

    def kernel(*refs):
        near_kernel(blocks, *refs)

    return pl.pallas_call(
        kernel,
        in_specs=[SMEM, SMEM] + [VMEM] * 5,
        out_specs=[VMEM, VMEM],
        out_shape=[
            jax.ShapeDtypeStruct((pairs, rows, 2 * PAIR), F32),
            jax.ShapeDtypeStruct((pairs, rows, PAIR), F32),
        ],
        compiler_params=pltpu.CompilerParams(vmem_limit_bytes=24 * 2**20),
        name="near_attend",
    )(gap_mask, reach, q, *own, *fast)


def far_kernel(grp, blocks, gap_ref, reach_ref, q_ref, kv_ref, acc_ref, max_ref, out_ref):
    rows = q_ref.shape[1]
    seen = window_of(gap_ref, reach_ref, rows, blocks, False)
    for i in range(2):
        p = 2 * grp + i
        keys, v = kv_ref[i], kv_ref[2 + i]
        va = jnp.concatenate([values_and_ones(v, h) for h in range(2)], axis=0)
        for t in range(rows // ROWS):
            part = pl.ds(t * ROWS, ROWS)
            q = q_ref[p, part]
            old = max_ref[p, part]
            scales, probs = [], []
            for h in range(2):
                s = jnp.where(seen, dot_t(one_head(q, h), keys), -1e30)
                before = old[:, h * HEAD : h * HEAD + 1]
                top = jnp.maximum(jnp.max(s, axis=-1, keepdims=True), before)
                scales.append(jnp.exp2(before - top))
                probs.append(jnp.exp2(s - top).astype(BF))
            acc = dot(jnp.concatenate(probs, axis=1), va)
            scale = spread(scales[0], scales[1], ROWS)
            old_acc = acc_ref[p, part]
            num = acc[:, :PAIR] + old_acc[:, :PAIR] * scale
            den = acc[:, PAIR:] + old_acc[:, PAIR:] * scale
            out_ref[part, i * PAIR : (i + 1) * PAIR] = (num / den).astype(BF)


def far_attend(grp, gap_mask, reach, q, kv, acc, top):
    pairs, rows, _ = q.shape
    blocks = gap_mask.shape[1]

    def kernel(*refs):
        far_kernel(grp, blocks, *refs)

    return pl.pallas_call(
        kernel,
        in_specs=[SMEM, SMEM] + [VMEM] * 4,
        out_specs=VMEM,
        out_shape=jax.ShapeDtypeStruct((rows, pairs // 2 * PAIR), BF),
        compiler_params=pltpu.CompilerParams(vmem_limit_bytes=24 * 2**20),
        name=f"far_attend{grp}",
    )(gap_mask, reach, q, kv, acc, top)


def middle_kernel(x_ref, a0_ref, a1_ref, w_ref, mid_ref, send_ref):
    half = a0_ref.shape[1]
    mid = x_ref[...].astype(F32) + dot(a0_ref[...], w_ref[:half]) + dot(a1_ref[...], w_ref[half:])
    mid_ref[...] = mid
    send_ref[...] = mid.astype(BF)


def middle_of(x, att0, att1, weights):
    rows, features = x.shape
    return pl.pallas_call(
        middle_kernel,
        in_specs=[VMEM] * 4,
        out_specs=[VMEM, VMEM],
        out_shape=[
            jax.ShapeDtypeStruct((rows, features), F32),
            jax.ShapeDtypeStruct((rows, features), BF),
        ],
        compiler_params=pltpu.CompilerParams(vmem_limit_bytes=16 * 2**20),
        name="middle",
    )(x, att0, att1, weights)


COLS = 16


def column_kernel(gap_ref, mid_ref, w_ref, out_ref, pack_ref):
    species, columns, features = mid_ref.shape
    hd = out_ref.shape[2]
    pairs = hd // PAIR
    n = rms(mid_ref[...].reshape(species * columns, features).astype(F32)).astype(BF)
    for j in range(3 * pairs // 2):
        out = dot(n, w_ref[:, 2 * j * PAIR : 2 * (j + 1) * PAIR])
        if j < pairs // 2:
            out = out * SCALE
        out = out.astype(BF).reshape(species, columns, 2 * PAIR)
        pack_ref[2 * j] = out[:, :, :PAIR]
        pack_ref[2 * j + 1] = out[:, :, PAIR:]
    block = lax.axis_index("ctx")
    rows = species * COLS
    qrow = lax.broadcasted_iota(jnp.int32, (rows, rows), 0)
    krow = lax.broadcasted_iota(jnp.int32, (rows, rows), 1)
    alive = jnp.zeros((rows, rows), jnp.int32)
    for t in range(species):
        alive = jnp.where(lax.div(krow, COLS) == t, gap_ref[t, block], alive)
    seen = (lax.rem(qrow, COLS) == lax.rem(krow, COLS)) & (alive == 1)
    seen = jnp.concatenate([seen, seen], axis=0)
    for j in range(columns // COLS):
        part = pl.ds(j * COLS, COLS)
        for p in range(pairs):
            q = pack_ref[p, :, part, :].reshape(rows, PAIR)
            k = pack_ref[pairs + p, :, part, :].reshape(rows, PAIR)
            v = pack_ref[2 * pairs + p, :, part, :].reshape(rows, PAIR)
            qs = jnp.concatenate([one_head(q, 0), one_head(q, 1)], axis=0)
            s = jnp.where(seen, dot_t(qs, k), -1e30)
            prob = jnp.exp2(s - jnp.max(s, axis=-1, keepdims=True)).astype(BF)
            prob = jnp.concatenate([prob[:rows], prob[rows:]], axis=1)
            va = jnp.concatenate([values_and_ones(v, 0), values_and_ones(v, 1)], axis=0)
            acc = dot(prob, va)
            att = (acc[:, :PAIR] / acc[:, PAIR:]).astype(BF)
            out_ref[:, part, p * PAIR : (p + 1) * PAIR] = att.reshape(species, COLS, PAIR)


def column_attend(gap_mask, mid, weights):
    species, columns, _ = mid.shape
    hd = weights.shape[1] // 3
    return pl.pallas_call(
        column_kernel,
        in_specs=[SMEM, VMEM, VMEM],
        out_specs=VMEM,
        out_shape=jax.ShapeDtypeStruct((species, columns, hd), BF),
        scratch_shapes=[pltpu.VMEM((3 * hd // PAIR, species, columns, PAIR), BF)],
        compiler_params=pltpu.CompilerParams(vmem_limit_bytes=24 * 2**20),
        name="column_attend",
    )(gap_mask, mid, weights)


def last_kernel(mid_ref, att_ref, w_ref, out_ref):
    out_ref[...] = (mid_ref[...] + dot(att_ref[...], w_ref[...])).astype(BF)


def last(mid, att, weights):
    rows, features = mid.shape
    hd = att.shape[1]
    tile = rows // 4
    return pl.pallas_call(
        last_kernel,
        grid=(rows // tile,),
        in_specs=[
            pl.BlockSpec((tile, features), lambda i: (i, 0)),
            pl.BlockSpec((tile, hd), lambda i: (i, 0)),
            pl.BlockSpec((hd, features), lambda i: (0, 0)),
        ],
        out_specs=pl.BlockSpec((tile, features), lambda i: (i, 0)),
        out_shape=jax.ShapeDtypeStruct((rows, features), BF),
        compiler_params=pltpu.CompilerParams(vmem_limit_bytes=16 * 2**20),
        name="last",
    )(mid, att, weights)


def body(tokens, gap_mask, window_reach, row_qkv, row_out, col_qkv, col_out):
    _, blocklen, features = tokens.shape
    hd = row_out.shape[0]
    blocks = lax.axis_size("ctx")
    species = lax.axis_size("species")
    near = [(i, i ^ 1) for i in range(blocks)]
    far = [(i, (i + 1 if i % 2 else i - 1) % blocks) for i in range(blocks)]
    x = tokens.reshape(blocklen, features)

    normed, kv0, kv1 = keyval(x, row_qkv)
    far0 = lax.ppermute(kv0, "ctx", far)
    fast0 = lax.ppermute(kv0, "ctx", near)
    fast1 = lax.ppermute(kv1, "ctx", near)
    far1 = lax.ppermute(kv1, "ctx", far)
    q = queries(normed, row_qkv)
    acc, top = near_attend(gap_mask, window_reach, q, (kv0, kv1), (fast0, fast1))
    att0 = far_attend(0, gap_mask, window_reach, q, far0, acc, top)
    att1 = far_attend(1, gap_mask, window_reach, q, far1, acc, top)
    mid, send = middle_of(x, att0, att1, row_out)

    columns = blocklen // species
    got = lax.all_to_all(send.reshape(species, columns, features), "species", 0, 0)
    col_att = column_attend(gap_mask, got, col_qkv)
    back = lax.all_to_all(col_att, "species", 0, 0)
    out = last(mid, back.reshape(blocklen, hd), col_out)
    return out.reshape(1, blocklen, features)


def solution(mesh):
    placed = (P("species", "ctx", None), P(), P(), P(), P(), P(), P())
    return jax.shard_map(
        body, mesh=mesh, in_specs=placed, out_specs=P("species", "ctx", None), check_vma=False
    )
```

time: 220 us -> 69.4 us (0.32); the launches traced: 218 us -> 69.2 us
  waiting for transfers between devices: 118 us -> 1.36 us
  blocking collectives: 0 us -> 39.3 us
  local copies, waits for them, and re-layouts: 40.1 us -> 3.15 us
  matrix products: 29.9 us -> 0 us
  Pallas kernels: 0 us -> 23 us
  between operations: 15.9 us -> 0.16 us
  other arithmetic: 13.4 us -> 0 us
    all_gather x1 -> x0, waiting for transfers between devices: 111 us -> none  [body(): lax.all_gather(col_packed[..., half_width:], 'species', axis=0, tiled=True)]
    all_to_all x0 -> x2, blocking collectives: none -> 39.3 us  [the longest x1 24.5 us: body(): lax.all_to_all(send.reshape(species, columns, features), 'species', 0, 0)]
    pallas_call x0 -> x8, Pallas kernels: none -> 23 us  [the longest x1 7.37 us: near_attend(): pl.pallas_call(kernel, in_specs=[SMEM, SMEM] + [VMEM] * 5, out_specs=[VME...]
    dot_general x5 -> x0, matrix products: 21.1 us -> none  [the longest x1 11.8 us: row_attend(): jnp.einsum('hqk,khd->qhd', weights, value_heads, preferred_element_type=j...]
    slice x9 -> x0, local copies, waits for them, and re-layouts: 20.8 us -> none  [the longest x1 5.74 us: column_attend(): keyval[..., :half_width].reshape(key_count, columns, head_count, HEAD)]
    unnamed x22 -> x18, local copies, waits for them, and re-layouts: 18 us -> 3.15 us
    sub x1 -> x0, matrix products: 8.78 us -> none  [softmax_last(): expsum = jnp.exp(scores - maxima)]
    unnamed x2 -> x0, other arithmetic: 6.03 us -> none
  transfers between devices with their start and end apart: 3 -> 4, of which waited for: 3 -> 1; matrix products, arithmetic and copies ran while one was open for 5% -> 0% of each run, Pallas kernels for 0% -> 16%
where the time goes in v1:
time: 69.4 us; the launch traced here: 69.2 us
  blocking collectives  39.3 us (57%)
  Pallas kernels  23 us (33%)
  local copies, waits for them, and re-layouts  3.15 us (5%)
  starting transfers between devices  2.33 us (3%)
  waiting for transfers between devices  1.36 us (2%)
    all_to_all x1, blocking collectives, body(): lax.all_to_all(send.reshape(species, columns, features), 'species', 0, 0)  24.5 us
    all_to_all x1, blocking collectives, body(): back = lax.all_to_all(col_att, 'species', 0, 0)  14.7 us
    pallas_call x1, Pallas kernels, near_attend(): pl.pallas_call(kernel, in_specs=[SMEM, SMEM] + [VMEM] * 5, out_specs=[VME...  7.37 us
    pallas_call x2, Pallas kernels, far_attend(): pl.pallas_call(kernel, in_specs=[SMEM, SMEM] + [VMEM] * 4, out_specs=VMEM...  5.9 us
    pallas_call x1, Pallas kernels, column_attend(): pl.pallas_call(column_kernel, in_specs=[SMEM, VMEM, VMEM], out_specs=VMEM...  3.39 us
    unnamed x18, local copies, waits for them, and re-layouts  3.15 us
    pallas_call x1, Pallas kernels, keyval(): pl.pallas_call(keyval_kernel, grid=(4,), in_specs=[pl.BlockSpec((rows, fe...  2.48 us
    pallas_call x1, Pallas kernels, last(): pl.pallas_call(last_kernel, grid=(rows // tile,), in_specs=[pl.BlockSpec(...  2.4 us
  transfers between devices with their start and end apart: 4, of which 1 were waited for; matrix products, arithmetic and copies ran while one was open for 0% of the time, Pallas kernels for 16%

profile of v1, /device:TPU:96, one launch (start us, length us, event | category | flops | bytes accessed | tf_op | source)
XLA Modules:
  0.0 69.2 jit_solution(18017442010944919886)
XLA Ops:
  0.0 1.9 %copy-done = bf16[1024,1536]{1,0:T(8,128)(2,1)S(1)} copy-done((bf16[1024,1536]{1,0:T(8,128)(2,1)S(1)}, bf16[1024,1536]{1,0:T(8,128)(2,1)}, u32[]{:S(2)}) %copy-start) | copy-done | bytes 3145752
  1.9 1.2 %copy-done.2 = bf16[1,512,1024]{2,1,0:T(8,128)(2,1)S(1)} copy-done((bf16[1,512,1024]{2,1,0:T(8,128)(2,1)S(1)}, bf16[1,512,1024]{2,1,0:T(8,128)(2,1)}, u32[]{:S(2)}) %copy-start.2) | copy-done | bytes 1048600
  3.1 2.5 %keyval.1 = (bf16[512,1024]{1,0:T(8,128)(2,1)S(1)}, bf16[4,512,128]{2,1,0:T(8,128)(2,1)S(1)}, bf16[4,512,128]{2,1,0:T(8,128)(2,1)S(1)}) custom-call(bf16[512,1024]{1,0:T(8,128)(2,1)S(1)} %bitcast.4, bf16[1024,1536]{1,0:T(8,128)(2,1)S(1)} %copy-done), custom_call_target="tpu_custom_call" | custom-call | tf_op jit(solution)/shard_map/keyval/pallas_call | solution.py:79
  5.6 0.0 copy-start.7
  5.6 0.0 copy-start.8
  5.6 0.1 collective-permute-start.1
  5.7 0.5 collective-permute-start.2
  6.2 0.0 collective-permute-start.3
  6.2 1.7 %collective-permute-start = (bf16[4,512,128]{2,1,0:T(8,128)(2,1)S(1)}, bf16[4,512,128]{2,1,0:T(8,128)(2,1)S(1)}, u32[]{:S(2)}, u32[]{:S(2)}) collective-permute-start(bf16[4,512,128]{2,1,0:T(8,128)(2,1)S(1)} %get-tuple-element.13.refs_3_), channel_id=1, source_target_pairs={{0,31},{1,2},{2,1},{3,4},{4,3},{5,6},{6,5},{7,8},{8,7},{9,10},{10,... | collective-permute-start | bytes 1572872 | tf_op jit(solution)/shard_map/ppermute | solution.py:341
  8.0 0.0 copy-done.1
  8.0 0.7 %queries.1.refs_2_ = bf16[4,512,128]{2,1,0:T(8,128)(2,1)S(1)} custom-call(bf16[512,1024]{1,0:T(8,128)(2,1)S(1)} %get-tuple-element.12.n_ref, bf16[1024,1536]{1,0:T(8,128)(2,1)S(1)} %copy-done.1), custom_call_target="tpu_custom_call" | custom-call | tf_op jit(solution)/shard_map/queries/pallas_call | solution.py:108
  8.7 0.0 collective-permute-done.1.refs_5_
  8.7 0.0 collective-permute-done.2.refs_6_
  8.7 0.0 copy-done.7
  8.7 0.0 copy-done.8
  8.7 7.4 %near_attend.1 = (f32[4,512,256]{2,1,0:T(8,128)S(1)}, f32[4,512,128]{2,1,0:T(8,128)S(1)}) custom-call(s32[8,32]{1,0:T(8,128)S(1)} %copy-done.7, s32[32]{0:T(128)S(1)} %copy-done.8, bf16[4,512,128]{2,1,0:T(8,128)(2,1)S(1)} %queries.1.refs_2_, bf16[4,512,128]{2,1,0:T(8,128)(2,1)S(1)} %get-tuple-element.13.refs_3_, ...), custom_call_target="tpu_custom_call" | custom-call | tf_op jit(solution)/shard_map/near_attend/pallas_call | solution.py:176
  16.1 0.0 collective-permute-done.3.refs_3_
  16.1 3.0 %far_attend1.1.a1_ref = bf16[512,256]{1,0:T(8,128)(2,1)S(1)} custom-call(s32[8,32]{1,0:T(8,128)S(1)} %copy-done.7, s32[32]{0:T(128)S(1)} %copy-done.8, bf16[4,512,128]{2,1,0:T(8,128)(2,1)S(1)} %queries.1.refs_2_, bf16[4,512,128]{2,1,0:T(8,128)(2,1)S(1)} %collective-permute-done.3.refs_3_, f32[4,512,256]{2,1,0:T(8,128)S(1)} %get-tuple-element.15.refs_4_, ...), custom_call_target="tpu_custom_call" | custom-call | tf_op jit(solution)/shard_map/far_attend1/pallas_call | solution.py:222
  19.1 0.0 copy-start.3
  19.1 0.0 copy-start.5
  19.1 1.3 %collective-permute-done.refs_3_ = bf16[4,512,128]{2,1,0:T(8,128)(2,1)S(1)} collective-permute-done((bf16[4,512,128]{2,1,0:T(8,128)(2,1)S(1)}, bf16[4,512,128]{2,1,0:T(8,128)(2,1)S(1)}, u32[]{:S(2)}, u32[]{:S(2)}) %collective-permute-start) | collective-permute-done | bytes 524320 | tf_op jit(solution)/shard_map/ppermute | solution.py:341
  20.5 2.9 %far_attend0.1.a0_ref = bf16[512,256]{1,0:T(8,128)(2,1)S(1)} custom-call(s32[8,32]{1,0:T(8,128)S(1)} %copy-done.7, s32[32]{0:T(128)S(1)} %copy-done.8, bf16[4,512,128]{2,1,0:T(8,128)(2,1)S(1)} %queries.1.refs_2_, bf16[4,512,128]{2,1,0:T(8,128)(2,1)S(1)} %collective-permute-done.refs_3_, f32[4,512,256]{2,1,0:T(8,128)S(1)} %get-tuple-element.15.refs_4_, ...), custom_call_target="tpu_custom_call" | custom-call | tf_op jit(solution)/shard_map/far_attend0/pallas_call | solution.py:222
  23.4 0.0 copy-done.3
  23.4 0.0 copy-done.5
  23.4 0.0 copy-start.4
  23.4 0.7 %middle.1 = (f32[512,1024]{1,0:T(8,128)S(1)}, bf16[512,1024]{1,0:T(8,128)(2,1)S(1)}) custom-call(bf16[512,1024]{1,0:T(8,128)(2,1)S(1)} %bitcast.5, bf16[512,256]{1,0:T(8,128)(2,1)S(1)} %far_attend0.1.a0_ref, bf16[512,256]{1,0:T(8,128)(2,1)S(1)} %far_attend1.1.a1_ref, bf16[512,1024]{1,0:T(8,128)(2,1)S(1)} %copy-done.5), custom_call_target="tpu_custom_call" | custom-call | tf_op jit(solution)/shard_map/middle/pallas_call | solution.py:241
  24.2 24.5 %all_to_all.10.mid_ref = bf16[8,64,1024]{2,1,0:T(8,128)(2,1)S(1)} all-to-all(bf16[8,64,1024]{2,1,0:T(8,128)(2,1)S(1)} %bitcast.7), channel_id=1, replica_groups=mesh['species'=8,'ctx'=32] {'species'}, dimensions={0} | all-to-all | bytes 2097152 | tf_op jit(solution)/shard_map/all_to_all | solution.py:352
  48.7 0.0 copy-done.4
  48.7 3.4 %column_attend.1 = bf16[8,64,512]{2,1,0:T(8,128)(2,1)S(1)} custom-call(s32[8,32]{1,0:T(8,128)S(1)} %copy-done.7, bf16[8,64,1024]{2,1,0:T(8,128)(2,1)S(1)} %all_to_all.10.mid_ref, bf16[1024,1536]{1,0:T(8,128)(2,1)S(1)} %copy-done.4), custom_call_target="tpu_custom_call" | custom-call | tf_op jit(solution)/shard_map/column_attend/pallas_call | solution.py:297
  52.1 14.7 %all_to_all.11 = bf16[8,64,512]{2,1,0:T(8,128)(2,1)S(1)} all-to-all(bf16[8,64,512]{2,1,0:T(8,128)(2,1)S(1)} %column_attend.1), channel_id=1, replica_groups=mesh['species'=8,'ctx'=32] {'species'}, dimensions={0} | all-to-all | bytes 1048576 | tf_op jit(solution)/shard_map/all_to_all | solution.py:354
  66.8 0.0 copy-done.6
  66.8 2.4 %last.1 = bf16[512,1024]{1,0:T(8,128)(2,1)} custom-call(f32[512,1024]{1,0:T(8,128)S(1)} %get-tuple-element.17.mid_ref, bf16[512,512]{1,0:T(8,128)(2,1)S(1)} %bitcast.6, bf16[512,1024]{1,0:T(8,128)(2,1)S(1)} %copy-done.6), custom_call_target="tpu_custom_call" | custom-call | tf_op jit(solution)/shard_map/last/pallas_call | solution.py:316
  (4 shorter events, 0.0 us)
Async XLA Ops:
  0.0 1.9 %copy-start = (bf16[1024,1536]{1,0:T(8,128)(2,1)S(1)}, bf16[1024,1536]{1,0:T(8,128)(2,1)}, u32[]{:S(2)}) copy-start(bf16[1024,1536]{1,0:T(8,128)(2,1)} %w_ref.6) | copy-start | bytes 9437188
  1.9 1.2 %copy-start.2 = (bf16[1,512,1024]{2,1,0:T(8,128)(2,1)S(1)}, bf16[1,512,1024]{2,1,0:T(8,128)(2,1)}, u32[]{:S(2)}) copy-start(bf16[1,512,1024]{2,1,0:T(8,128)(2,1)} %param.7) | copy-start | bytes 3145732
  3.1 4.9 %copy-start.1 = (bf16[1024,1536]{1,0:T(8,128)(2,1)S(1)}, bf16[1024,1536]{1,0:T(8,128)(2,1)}, u32[]{:S(2)}) copy-start(bf16[1024,1536]{1,0:T(8,128)(2,1)} %w_ref.6) | copy-start | bytes 9437188
  5.6 3.1 %copy-start.7 = (s32[8,32]{1,0:T(8,128)S(1)}, s32[8,32]{1,0:T(8,128)}, u32[]{:S(2)}) copy-start(s32[8,32]{1,0:T(8,128)} %gap_ref.1) | copy-start | bytes 3076
  5.6 3.1 %copy-start.8 = (s32[32]{0:T(128)S(1)}, s32[32]{0:T(128)}, u32[]{:S(2)}) copy-start(s32[32]{0:T(128)} %refs_1_.5) | copy-start | bytes 388
  5.6 3.1 %collective-permute-start.1 = (bf16[4,512,128]{2,1,0:T(8,128)(2,1)S(1)}, bf16[4,512,128]{2,1,0:T(8,128)(2,1)S(1)}, u32[]{:S(2)}, u32[]{:S(2)}) collective-permute-start(bf16[4,512,128]{2,1,0:T(8,128)(2,1)S(1)} %get-tuple-element.13.refs_3_), channel_id=1, source_target_pairs={{0,1},{1,0},{2,3},{3,2},{4,5},{5,4},{6,7},{7,6},{8,9},{9,8},{10,11... | collective-permute-start | bytes 1572872 | tf_op jit(solution)/shard_map/ppermute | solution.py:342
  5.7 3.0 %collective-permute-start.2 = (bf16[4,512,128]{2,1,0:T(8,128)(2,1)S(1)}, bf16[4,512,128]{2,1,0:T(8,128)(2,1)S(1)}, u32[]{:S(2)}, u32[]{:S(2)}) collective-permute-start(bf16[4,512,128]{2,1,0:T(8,128)(2,1)S(1)} %get-tuple-element.14.refs_4_), channel_id=1, source_target_pairs={{0,1},{1,0},{2,3},{3,2},{4,5},{5,4},{6,7},{7,6},{8,9},{9,8},{10,11... | collective-permute-start | bytes 1572872 | tf_op jit(solution)/shard_map/ppermute | solution.py:343
  6.2 9.9 %collective-permute-start.3 = (bf16[4,512,128]{2,1,0:T(8,128)(2,1)S(1)}, bf16[4,512,128]{2,1,0:T(8,128)(2,1)S(1)}, u32[]{:S(2)}, u32[]{:S(2)}) collective-permute-start(bf16[4,512,128]{2,1,0:T(8,128)(2,1)S(1)} %get-tuple-element.14.refs_4_), channel_id=1, source_target_pairs={{0,31},{1,2},{2,1},{3,4},{4,3},{5,6},{6,5},{7,8},{8,7},{9,10},{10,... | collective-permute-start | bytes 1572872 | tf_op jit(solution)/shard_map/ppermute | solution.py:344
  6.2 14.2 %collective-permute-start = (bf16[4,512,128]{2,1,0:T(8,128)(2,1)S(1)}, bf16[4,512,128]{2,1,0:T(8,128)(2,1)S(1)}, u32[]{:S(2)}, u32[]{:S(2)}) collective-permute-start(bf16[4,512,128]{2,1,0:T(8,128)(2,1)S(1)} %get-tuple-element.13.refs_3_), channel_id=1, source_target_pairs={{0,31},{1,2},{2,1},{3,4},{4,3},{5,6},{6,5},{7,8},{8,7},{9,10},{10,... | collective-permute-start | bytes 1572872 | tf_op jit(solution)/shard_map/ppermute | solution.py:341
  19.1 4.3 %copy-start.3 = (bf16[1,512,1024]{2,1,0:T(8,128)(2,1)S(1)}, bf16[1,512,1024]{2,1,0:T(8,128)(2,1)}, u32[]{:S(2)}) copy-start(bf16[1,512,1024]{2,1,0:T(8,128)(2,1)} %param.7) | copy-start | bytes 3145732
  19.1 4.3 %copy-start.5 = (bf16[512,1024]{1,0:T(8,128)(2,1)S(1)}, bf16[512,1024]{1,0:T(8,128)(2,1)}, u32[]{:S(2)}) copy-start(bf16[512,1024]{1,0:T(8,128)(2,1)} %w_ref.7) | copy-start | bytes 3145732
  23.4 25.3 %copy-start.4 = (bf16[1024,1536]{1,0:T(8,128)(2,1)S(1)}, bf16[1024,1536]{1,0:T(8,128)(2,1)}, u32[]{:S(2)}) copy-start(bf16[1024,1536]{1,0:T(8,128)(2,1)} %w_ref.8) | copy-start | bytes 9437188
  48.7 18.1 %copy-start.6 = (bf16[512,1024]{1,0:T(8,128)(2,1)S(1)}, bf16[512,1024]{1,0:T(8,128)(2,1)}, u32[]{:S(2)}) copy-start(bf16[512,1024]{1,0:T(8,128)(2,1)} %w_ref.9) | copy-start | bytes 3145732

commit v2 on v1

v2 whole, which is shorter than its diff:
```python
import math

import jax
import jax.numpy as jnp
from jax import lax
from jax.experimental import pallas as pl
from jax.experimental.pallas import tpu as pltpu
from jax.sharding import PartitionSpec as P

HEAD = 64
PAIR = 2 * HEAD
ROWS = 128
COLS = 16
FAR = ((0, 1, 2), (3,))
SCALE = HEAD ** (-0.5) / math.log(2.0)
BF = jnp.bfloat16
F32 = jnp.float32
VMEM = pl.BlockSpec(memory_space=pltpu.VMEM)
SMEM = pl.BlockSpec(memory_space=pltpu.SMEM)
HBM = pl.BlockSpec(memory_space=pltpu.HBM)


def dot(a, b):
    return jnp.dot(a, b, preferred_element_type=F32)


def dot_t(a, b):
    return lax.dot_general(a, b, (((1,), (1,)), ((), ())), preferred_element_type=F32)


def rms(values):
    return values * lax.rsqrt(jnp.mean(values * values, axis=-1, keepdims=True) + 1e-06)


def lower_half(rows):
    return lax.broadcasted_iota(jnp.int32, (rows, PAIR), 1) < HEAD


def one_head(pair, head):
    low = lower_half(pair.shape[0])
    keep = low if head == 0 else ~low
    return jnp.where(keep, pair, jnp.zeros_like(pair))


def values_and_ones(pair, head):
    return jnp.concatenate([one_head(pair, head), one_head(jnp.ones_like(pair), head)], axis=1)


def cost(flops, bytes_accessed):
    return pl.CostEstimate(flops=flops, bytes_accessed=bytes_accessed, transcendentals=0)


def window_of(gap_ref, reach_ref, blocklen, blocks, fast):
    block = lax.axis_index("ctx")
    species = lax.axis_index("species")
    odd = lax.rem(block, 2)
    before = odd == 1 if fast else odd == 0
    other = jnp.where(before, lax.rem(block + blocks - 1, blocks), lax.rem(block + 1, blocks))
    reach = reach_ref[block]
    low = jnp.where(before, blocklen - reach, 0)
    high = jnp.where(before, blocklen, reach)
    high = jnp.where(gap_ref[species, other] == 1, high, 0)
    cols = lax.broadcasted_iota(jnp.int32, (8, blocklen), 1)
    return jnp.where((cols >= low) & (cols < high), 1.0, 0.0)


def keyval_kernel(x_hbm, w_hbm, x_ref, n_ref, wq_ref, kv_ref, *refs):
    far_refs = refs[: len(FAR)]
    w_ref, xsem, wsem, qsem = refs[len(FAR) :]
    rows = x_ref.shape[0]
    hd = wq_ref.shape[1]
    pairs = hd // PAIR
    parts = xsem.shape[0]
    tile = rows // parts
    xs = [
        pltpu.make_async_copy(
            x_hbm.at[pl.ds(i * tile, tile)], x_ref.at[pl.ds(i * tile, tile)], xsem.at[i]
        )
        for i in range(parts)
    ]
    ws = [
        pltpu.make_async_copy(
            w_hbm.at[:, pl.ds(hd + i * hd // 2, hd // 2)],
            w_ref.at[:, pl.ds(i * hd // 2, hd // 2)],
            wsem.at[i],
        )
        for i in range(4)
    ]
    wq = pltpu.make_async_copy(w_hbm.at[:, pl.ds(0, hd)], wq_ref, qsem)
    for copy in xs + ws:
        copy.start()
    wq.start()
    for i in range(parts):
        xs[i].wait()
        part = pl.ds(i * tile, tile)
        n_ref[part] = rms(x_ref[part].astype(F32)).astype(BF)
    for copy in ws:
        copy.wait()
    out = dot(n_ref[...], w_ref[...]).astype(BF)
    for p in range(2 * pairs):
        kv_ref[p] = out[:, p * PAIR : (p + 1) * PAIR]
    for far_ref, group in zip(far_refs, FAR):
        for i, p in enumerate(group):
            far_ref[i] = out[:, p * PAIR : (p + 1) * PAIR]
            far_ref[len(group) + i] = out[:, hd + p * PAIR : hd + (p + 1) * PAIR]
    wq.wait()


def keyval(x, weights):
    rows, features = x.shape
    hd = weights.shape[1] // 3
    pairs = hd // PAIR
    out = pl.pallas_call(
        keyval_kernel,
        in_specs=[HBM] * 2,
        out_specs=[VMEM] * (4 + len(FAR)),
        out_shape=[
            jax.ShapeDtypeStruct((rows, features), BF),
            jax.ShapeDtypeStruct((rows, features), BF),
            jax.ShapeDtypeStruct((features, hd), BF),
            jax.ShapeDtypeStruct((2 * pairs, rows, PAIR), BF),
            *[jax.ShapeDtypeStruct((2 * len(group), rows, PAIR), BF) for group in FAR],
        ],
        scratch_shapes=[
            pltpu.VMEM((features, 2 * hd), BF),
            pltpu.SemaphoreType.DMA((4,)),
            pltpu.SemaphoreType.DMA((4,)),
            pltpu.SemaphoreType.DMA,
        ],
        compiler_params=pltpu.CompilerParams(vmem_limit_bytes=48 * 2**20),
        cost_estimate=cost(2 * rows * features * 2 * hd, 6 * 2**20),
        name="keyval",
    )(x, weights)
    return *out[:4], out[4:]


def query_kernel(gap_ref, reach_ref, n_ref, w_ref, q_ref, mask_ref, alive_ref):
    out = (dot(n_ref[...], w_ref[...]) * SCALE).astype(BF)
    for p in range(q_ref.shape[0]):
        q_ref[p] = out[:, p * PAIR : (p + 1) * PAIR]
    species, blocks = gap_ref.shape
    for i in range(2):
        mask_ref[i] = window_of(gap_ref, reach_ref, n_ref.shape[0], blocks, i == 0)
    lanes = lax.broadcasted_iota(jnp.int32, alive_ref.shape, 1)
    alive = jnp.zeros(alive_ref.shape, jnp.int32)
    for t in range(species):
        alive = jnp.where(lax.div(lanes, COLS) == t, gap_ref[t, lax.axis_index("ctx")], alive)
    alive_ref[...] = alive


def queries(gap_mask, reach, normed, weights):
    rows, features = normed.shape
    hd = weights.shape[1]
    species = gap_mask.shape[0]
    return pl.pallas_call(
        query_kernel,
        in_specs=[SMEM, SMEM, VMEM, VMEM],
        out_specs=[VMEM] * 3,
        out_shape=[
            jax.ShapeDtypeStruct((hd // PAIR, rows, PAIR), BF),
            jax.ShapeDtypeStruct((2, 8, rows), F32),
            jax.ShapeDtypeStruct((8, species * COLS), jnp.int32),
        ],
        compiler_params=pltpu.CompilerParams(vmem_limit_bytes=16 * 2**20),
        cost_estimate=cost(2 * rows * features * hd, 2**20),
        name="queries",
    )(gap_mask, reach, normed, weights)


def near_kernel(mask_ref, q_ref, own, fast, acc_ref, max_ref):
    pairs, rows, _ = q_ref.shape
    seen = mask_ref[0, :1] > 0.5

    def scores(p, t):
        q = q_ref[p, pl.ds(t * ROWS, ROWS)]
        heads = [one_head(q, h) for h in range(2)]
        return [(dot_t(q, own[p]), dot_t(q, fast[p])) for q in heads]

    def finish(p, t, found, va):
        part = pl.ds(t * ROWS, ROWS)
        probs = []
        for h, (so, sf) in enumerate(found):
            sf = jnp.where(seen, sf, -1e30)
            top = jnp.maximum(
                jnp.max(so, axis=-1, keepdims=True), jnp.max(sf, axis=-1, keepdims=True)
            )
            max_ref[2 * p + h, part] = jnp.broadcast_to(top, (ROWS, PAIR))
            probs += [jnp.exp2(so - top).astype(BF), jnp.exp2(sf - top).astype(BF)]
        acc_ref[p, part] = dot(jnp.concatenate(probs, axis=1), va)

    late = None
    for p in range(pairs):
        vals = (own[pairs + p], fast[pairs + p])
        va = jnp.concatenate([values_and_ones(v, h) for h in range(2) for v in vals], axis=0)
        for t in range(rows // ROWS):
            found = scores(p, t)
            if late is not None:
                finish(*late)
            late = (p, t, found, va)
    finish(*late)


def near_attend(mask, q, own, fast):
    pairs, rows, _ = q.shape
    return pl.pallas_call(
        near_kernel,
        in_specs=[VMEM] * 4,
        out_specs=[VMEM, VMEM],
        out_shape=[
            jax.ShapeDtypeStruct((pairs, rows, 2 * PAIR), F32),
            jax.ShapeDtypeStruct((2 * pairs, rows, PAIR), F32),
        ],
        compiler_params=pltpu.CompilerParams(vmem_limit_bytes=24 * 2**20),
        cost_estimate=cost(32 * rows * rows * PAIR * pairs, 2**23),
        name="near_attend",
    )(mask, q, own, fast)


def far_kernel(group, mask_ref, q_ref, kv_ref, acc_ref, max_ref, *refs):
    out_ref = refs[-1]
    rows = q_ref.shape[1]
    seen = mask_ref[1, :1] > 0.5

    def scores(i, t):
        q = q_ref[group[i], pl.ds(t * ROWS, ROWS)]
        return [dot_t(one_head(q, h), kv_ref[i]) for h in range(2)]

    def finish(i, t, found, va):
        p = group[i]
        part = pl.ds(t * ROWS, ROWS)
        scales, probs = [], []
        for h, s in enumerate(found):
            s = jnp.where(seen, s, -1e30)
            before = max_ref[2 * p + h, part]
            top = jnp.maximum(jnp.max(s, axis=-1, keepdims=True), before)
            scales.append(jnp.exp2(before - top))
            probs.append(jnp.exp2(s - jnp.concatenate([top] * (rows // PAIR), axis=1)).astype(BF))
        acc = dot(jnp.concatenate(probs, axis=1), va)
        scale = jnp.where(lower_half(ROWS), scales[0], scales[1])
        old = acc_ref[p, part]
        num = acc[:, :PAIR] + old[:, :PAIR] * scale
        den = acc[:, PAIR:] + old[:, PAIR:] * scale
        out_ref[part, p * PAIR : (p + 1) * PAIR] = (num / den).astype(BF)

    late = None
    for i in range(len(group)):
        vals = kv_ref[len(group) + i]
        va = jnp.concatenate([values_and_ones(vals, h) for h in range(2)], axis=0)
        for t in range(rows // ROWS):
            found = scores(i, t)
            if late is not None:
                finish(*late)
            late = (i, t, found, va)
    finish(*late)


def far_attend(group, mask, q, kv, acc, top, att):
    pairs, rows, _ = q.shape

    def kernel(*refs):
        far_kernel(group, *refs)

    return pl.pallas_call(
        kernel,
        in_specs=[VMEM] * (5 + len(att)),
        out_specs=VMEM,
        out_shape=jax.ShapeDtypeStruct((rows, pairs * PAIR), BF),
        input_output_aliases={5: 0} if att else {},
        compiler_params=pltpu.CompilerParams(vmem_limit_bytes=24 * 2**20),
        cost_estimate=cost(16 * rows * rows * PAIR * len(group), 2**21),
        name=f"far_attend{group[0]}",
    )(mask, q, kv, acc, top, *att)


def middle_kernel(x_ref, att_ref, w_ref, mid_ref, send_ref):
    mid = x_ref[...].astype(F32) + dot(att_ref[...], w_ref[...])
    mid_ref[...] = mid
    send_ref[...] = mid.astype(BF)


def middle_of(x, att, weights):
    rows, features = x.shape
    return pl.pallas_call(
        middle_kernel,
        in_specs=[VMEM] * 3,
        out_specs=[VMEM, VMEM],
        out_shape=[
            jax.ShapeDtypeStruct((rows, features), F32),
            jax.ShapeDtypeStruct((rows, features), BF),
        ],
        compiler_params=pltpu.CompilerParams(vmem_limit_bytes=16 * 2**20),
        cost_estimate=cost(2 * rows * features * weights.shape[0], 2**22),
        name="middle",
    )(x, att, weights)


def column_kernel(alive_ref, mid_ref, w_ref, out_ref, pack_ref):
    species, columns, features = mid_ref.shape
    hd = out_ref.shape[2]
    pairs = hd // PAIR
    n = rms(mid_ref[...].reshape(species * columns, features).astype(F32)).astype(BF)
    for j in range(3):
        out = dot(n, w_ref[:, j * hd : (j + 1) * hd])
        if j == 0:
            out = out * SCALE
        out = out.astype(BF).reshape(species, columns, hd)
        for p in range(pairs):
            pack_ref[j * pairs + p] = out[:, :, p * PAIR : (p + 1) * PAIR]
    rows = species * COLS
    qrow = lax.broadcasted_iota(jnp.int32, (rows, rows), 0)
    krow = lax.broadcasted_iota(jnp.int32, (rows, rows), 1)
    seen = (lax.rem(qrow, COLS) == lax.rem(krow, COLS)) & (alive_ref[:1] == 1)
    seen = jnp.concatenate([seen, seen], axis=0)
    for j in range(columns // COLS):
        part = pl.ds(j * COLS, COLS)
        for p in range(pairs):
            q = pack_ref[p, :, part, :].reshape(rows, PAIR)
            k = pack_ref[pairs + p, :, part, :].reshape(rows, PAIR)
            v = pack_ref[2 * pairs + p, :, part, :].reshape(rows, PAIR)
            qs = jnp.concatenate([one_head(q, 0), one_head(q, 1)], axis=0)
            s = jnp.where(seen, dot_t(qs, k), -1e30)
            prob = jnp.exp2(s - jnp.max(s, axis=-1, keepdims=True)).astype(BF)
            prob = jnp.concatenate([prob[:rows], prob[rows:]], axis=1)
            va = jnp.concatenate([values_and_ones(v, 0), values_and_ones(v, 1)], axis=0)
            acc = dot(prob, va)
            att = (acc[:, :PAIR] / acc[:, PAIR:]).astype(BF)
            out_ref[:, part, p * PAIR : (p + 1) * PAIR] = att.reshape(species, COLS, PAIR)


def column_attend(alive, mid, weights):
    species, columns, _ = mid.shape
    hd = weights.shape[1] // 3
    return pl.pallas_call(
        column_kernel,
        in_specs=[VMEM] * 3,
        out_specs=VMEM,
        out_shape=jax.ShapeDtypeStruct((species, columns, hd), BF),
        scratch_shapes=[pltpu.VMEM((3 * hd // PAIR, species, columns, PAIR), BF)],
        compiler_params=pltpu.CompilerParams(vmem_limit_bytes=24 * 2**20),
        name="column_attend",
    )(alive, mid, weights)


def last_kernel(mid_ref, att_ref, w_ref, out_ref):
    tile = out_ref.shape[0]
    part = pl.ds(pl.multiple_of(pl.program_id(0) * tile, tile), tile)
    out_ref[...] = (mid_ref[part] + dot(att_ref[part], w_ref[...])).astype(BF)


def last(mid, att, weights):
    rows, features = mid.shape
    tile = rows // 2
    return pl.pallas_call(
        last_kernel,
        grid=(rows // tile,),
        in_specs=[VMEM] * 3,
        out_specs=pl.BlockSpec((tile, features), lambda i: (i, 0)),
        out_shape=jax.ShapeDtypeStruct((rows, features), BF),
        compiler_params=pltpu.CompilerParams(vmem_limit_bytes=16 * 2**20),
        name="last",
    )(mid, att, weights)


def body(tokens, gap_mask, window_reach, row_qkv, row_out, col_qkv, col_out):
    _, blocklen, features = tokens.shape
    hd = row_out.shape[0]
    blocks = lax.axis_size("ctx")
    species = lax.axis_size("species")
    columns = blocklen // species
    near = [(i, i ^ 1) for i in range(blocks)]
    far = [(i, (i + 1 if i % 2 else i - 1) % blocks) for i in range(blocks)]
    x = tokens.reshape(blocklen, features)

    def by_column(array):
        return lax.all_to_all(array.reshape(species, columns, array.shape[1]), "species", 0, 0)

    x, normed, wq, own, sends = keyval(x, row_qkv)
    q, mask, alive = queries(gap_mask, window_reach, normed, wq)
    q, last_send = lax.optimization_barrier((q, sends[-1]))
    fars = [lax.ppermute(kv, "ctx", far) for kv in (*sends[:-1], last_send)]
    fast = lax.ppermute(own, "ctx", near)
    acc, top = near_attend(mask, q, own, fast)
    att = []
    for group, kv in zip(FAR, fars):
        att = [far_attend(group, mask, q, kv, acc, top, att)]
    mid, send = middle_of(x, att[0], row_out)
    col_att = column_attend(alive, by_column(send), col_qkv)
    back = lax.all_to_all(col_att, "species", 0, 0)
    out = last(mid, back.reshape(blocklen, hd), col_out)
    return out.reshape(1, blocklen, features)


def solution(mesh):
    placed = (P("species", "ctx", None), P(), P(), P(), P(), P(), P())
    return jax.shard_map(
        body, mesh=mesh, in_specs=placed, out_specs=P("species", "ctx", None), check_vma=False
    )
```

time: 69.4 us -> 63.4 us (0.914)
  Pallas kernels: 23 us -> 18 us
  local copies, waits for them, and re-layouts: 3.15 us -> 0.02 us
  waiting for transfers between devices: 1.36 us -> 3.71 us
    pallas_call x8, Pallas kernels: 23 us -> 18 us  [the longest x1 5.08 us: near_attend(): pl.pallas_call(near_kernel, in_specs=[VMEM] * 4, out_specs=[VMEM, VMEM],...]
    unnamed x18 -> x10, local copies, waits for them, and re-layouts: 3.15 us -> 0.02 us
    ppermute x4 -> x3, waiting for transfers between devices: 1.36 us -> 3.71 us  [the longest x2 3.71 us: body(): fars = [lax.ppermute(kv, 'ctx', far) for kv in (*sends[:-1], last_send)]]
    ppermute x4 -> x3, starting transfers between devices: 2.33 us -> 2.01 us  [the longest x2 1.92 us: body(): fars = [lax.ppermute(kv, 'ctx', far) for kv in (*sends[:-1], last_send)]]
  transfers between devices with their start and end apart: 4 -> 3, of which waited for: 1 -> 2; matrix products, arithmetic and copies ran while one was open for 0% -> 0% of each run, Pallas kernels for 16% -> 14%
where the time goes in v2:
time: 63.4 us; the launch traced here: 63.3 us
  blocking collectives  39.4 us (62%)
  Pallas kernels  18 us (28%)
  waiting for transfers between devices  3.71 us (6%)
  starting transfers between devices  2.01 us (3%)
    all_to_all x1, blocking collectives, by_column(): lax.all_to_all(array.reshape(species, columns, array.shape[1]), 'species'...  24.7 us
    all_to_all x1, blocking collectives, body(): back = lax.all_to_all(col_att, 'species', 0, 0)  14.7 us
    pallas_call x1, Pallas kernels, near_attend(): pl.pallas_call(near_kernel, in_specs=[VMEM] * 4, out_specs=[VMEM, VMEM],...  5.08 us
    ppermute x2, waiting for transfers between devices, body(): fars = [lax.ppermute(kv, 'ctx', far) for kv in (*sends[:-1], last_send)]  3.71 us
    pallas_call x1, Pallas kernels, keyval(): pl.pallas_call(keyval_kernel, in_specs=[HBM] * 2, out_specs=[VMEM] * (4 +...  3.21 us
    pallas_call x2, Pallas kernels, far_attend(): pl.pallas_call(kernel, in_specs=[VMEM] * (5 + len(att)), out_specs=VMEM,...  3.21 us
    pallas_call x1, Pallas kernels, column_attend(): pl.pallas_call(column_kernel, in_specs=[VMEM] * 3, out_specs=VMEM, out_sh...  2.79 us
    ppermute x2, starting transfers between devices, body(): fars = [lax.ppermute(kv, 'ctx', far) for kv in (*sends[:-1], last_send)]  1.92 us
  transfers between devices with their start and end apart: 3, of which 2 were waited for; matrix products, arithmetic and copies ran while one was open for 0% of the time, Pallas kernels for 14%

profile of v2, /device:TPU:96, one launch (start us, length us, event | category | flops | bytes accessed | tf_op | source)
XLA Modules:
  0.0 63.3 jit_solution(13431300348714518681)
XLA Ops:
  0.0 0.0 copy-start.3
  0.0 0.0 copy-start.4
  0.0 3.2 %keyval.1 = (bf16[512,1024]{1,0:T(8,128)(2,1)S(1)}, bf16[512,1024]{1,0:T(8,128)(2,1)S(1)}, bf16[1024,512]{1,0:T(8,128)(2,1)S(1)}, bf16[8,512,128]{2,1,0:T(8,128)...) custom-call(bf16[512,1024]{1,0:T(8,128)(2,1)} %bitcast.6, bf16[1024,1536]{1,0:T(8,128)(2,1)} %w_hbm.1), custom_call_target="tpu_custom_call" | custom-call | flops 1073741824 | bytes 6291456 | tf_op jit(solution)/shard_map/keyval/pallas_call | solution.py:113
  3.2 0.1 collective-permute-start.1
  3.3 0.2 collective-permute-start.2
  3.5 0.0 copy-done.3
  3.5 0.0 copy-done.4
  3.5 1.3 %queries.1 = (bf16[4,512,128]{2,1,0:T(8,128)(2,1)S(1)}, f32[2,8,512]{2,1,0:T(8,128)S(1)}, s32[8,128]{1,0:T(8,128)S(1)}) custom-call(s32[8,32]{1,0:T(8,128)S(1)} %copy-done.3, s32[32]{0:T(128)S(1)} %copy-done.4, bf16[512,1024]{1,0:T(8,128)(2,1)S(1)} %get-tuple-element.21.n_ref, bf16[1024,512]{1,0:T(8,128)(2,1)S(1)} %get-tuple-element.22.w_ref), custom_call_target="tpu_custom_call" | custom-call | flops 536870912 | bytes 1048576 | tf_op jit(solution)/shard_map/queries/pallas_call | solution.py:155
  4.9 1.7 %collective-permute-start = (bf16[2,512,128]{2,1,0:T(8,128)(2,1)S(1)}, bf16[2,512,128]{2,1,0:T(8,128)(2,1)S(1)}, u32[]{:S(2)}, u32[]{:S(2)}) collective-permute-start(bf16[2,512,128]{2,1,0:T(8,128)(2,1)S(1)} %get-tuple-element.27), channel_id=1, source_target_pairs={{0,31},{1,2},{2,1},{3,4},{4,3},{5,6},{6,5},{7,8},{8,7},{9,10},{10,... | collective-permute-start | bytes 786440 | tf_op jit(solution)/shard_map/ppermute | solution.py:380
  6.6 0.0 collective-permute-done.1.fast
  6.6 5.1 %near_attend.1 = (f32[4,512,256]{2,1,0:T(8,128)S(1)}, f32[8,512,128]{2,1,0:T(8,128)S(1)}) custom-call(f32[2,8,512]{2,1,0:T(8,128)S(1)} %get-tuple-element.23.mask_ref.refs_0_, bf16[4,512,128]{2,1,0:T(8,128)(2,1)S(1)} %get-tuple-element.26.q_ref.refs_1_, bf16[8,512,128]{2,1,0:T(8,128)(2,1)S(1)} %get-tuple-element.28.own, ...), custom_call_target="tpu_custom_call" | custom-call | flops 4294967296 | bytes 8388608 | tf_op jit(solution)/shard_map/near_attend/pallas_call | solution.py:205
  11.7 3.2 %collective-permute-done.2.refs_2_ = bf16[6,512,128]{2,1,0:T(8,128)(2,1)S(1)} collective-permute-done((bf16[6,512,128]{2,1,0:T(8,128)(2,1)S(1)}, bf16[6,512,128]{2,1,0:T(8,128)(2,1)S(1)}, u32[]{:S(2)}, u32[]{:S(2)}) %collective-permute-start.2) | collective-permute-done | bytes 786464 | tf_op jit(solution)/shard_map/ppermute | solution.py:380
  14.8 2.3 %far_attend0.1.refs_5_ = bf16[512,512]{1,0:T(8,128)(2,1)S(1)} custom-call(f32[2,8,512]{2,1,0:T(8,128)S(1)} %get-tuple-element.23.mask_ref.refs_0_, bf16[4,512,128]{2,1,0:T(8,128)(2,1)S(1)} %get-tuple-element.26.q_ref.refs_1_, bf16[6,512,128]{2,1,0:T(8,128)(2,1)S(1)} %collective-permute-done.2.refs_2_, f32[4,512,256]{2,1,0:T(8,128)S(1)} %get-tuple-element.29.refs_3_, ...), custom_call_target="tpu_custom_call" | custom-call | flops 1610612736 | bytes 2097152 | tf_op jit(solution)/shard_map/far_attend0/pallas_call | solution.py:263
  17.1 0.0 copy-start.1
  17.1 0.5 collective-permute-done.refs_2_
  17.6 1.0 %far_attend3.1.att_ref = bf16[512,512]{1,0:T(8,128)(2,1)S(1)} custom-call(f32[2,8,512]{2,1,0:T(8,128)S(1)} %get-tuple-element.23.mask_ref.refs_0_, bf16[4,512,128]{2,1,0:T(8,128)(2,1)S(1)} %get-tuple-element.26.q_ref.refs_1_, bf16[2,512,128]{2,1,0:T(8,128)(2,1)S(1)} %collective-permute-done.refs_2_, ...), custom_call_target="tpu_custom_call", output_to_operand_aliasing={{}: (5, {})} | custom-call | flops 536870912 | bytes 2097152 | tf_op jit(solution)/shard_map/far_attend3/pallas_call | solution.py:263
  18.6 0.0 copy-done.1
  18.6 0.0 copy-start
  18.6 0.7 %middle.1 = (f32[512,1024]{1,0:T(8,128)S(1)}, bf16[512,1024]{1,0:T(8,128)(2,1)S(1)}) custom-call(bf16[512,1024]{1,0:T(8,128)(2,1)S(1)} %get-tuple-element.20.x_ref, bf16[512,512]{1,0:T(8,128)(2,1)S(1)} %far_attend3.1.att_ref, bf16[512,1024]{1,0:T(8,128)(2,1)S(1)} %copy-done.1), custom_call_target="tpu_custom_call" | custom-call | flops 536870912 | bytes 4194304 | tf_op jit(solution)/shard_map/middle/pallas_call | solution.py:283
  19.3 24.7 %all_to_all.10.mid_ref = bf16[8,64,1024]{2,1,0:T(8,128)(2,1)S(1)} all-to-all(bf16[8,64,1024]{2,1,0:T(8,128)(2,1)S(1)} %bitcast.5), channel_id=1, replica_groups=mesh['species'=8,'ctx'=32] {'species'}, dimensions={0} | all-to-all | bytes 2097152 | tf_op jit(solution)/shard_map/all_to_all | solution.py:375
  44.0 0.0 copy-done
  44.0 0.0 copy-start.2
  44.0 2.8 %column_attend.1 = bf16[8,64,512]{2,1,0:T(8,128)(2,1)S(1)} custom-call(s32[8,128]{1,0:T(8,128)S(1)} %get-tuple-element.33.alive_ref, bf16[8,64,1024]{2,1,0:T(8,128)(2,1)S(1)} %all_to_all.10.mid_ref, bf16[1024,1536]{1,0:T(8,128)(2,1)S(1)} %copy-done), custom_call_target="tpu_custom_call" | custom-call | tf_op jit(solution)/shard_map/column_attend/pallas_call | solution.py:333
  46.8 14.7 %all_to_all.11 = bf16[8,64,512]{2,1,0:T(8,128)(2,1)S(1)} all-to-all(bf16[8,64,512]{2,1,0:T(8,128)(2,1)S(1)} %column_attend.1), channel_id=1, replica_groups=mesh['species'=8,'ctx'=32] {'species'}, dimensions={0} | all-to-all | bytes 1048576 | tf_op jit(solution)/shard_map/all_to_all | solution.py:388
  61.6 0.0 copy-done.2
  61.6 1.7 %last.1 = bf16[512,1024]{1,0:T(8,128)(2,1)} custom-call(f32[512,1024]{1,0:T(8,128)S(1)} %get-tuple-element.32.mid_ref, bf16[512,512]{1,0:T(8,128)(2,1)S(1)} %bitcast.4, bf16[512,1024]{1,0:T(8,128)(2,1)S(1)} %copy-done.2), custom_call_target="tpu_custom_call" | custom-call | tf_op jit(solution)/shard_map/last/pallas_call | solution.py:353
Async XLA Ops:
  0.0 3.5 %copy-start.3 = (s32[8,32]{1,0:T(8,128)S(1)}, s32[8,32]{1,0:T(8,128)}, u32[]{:S(2)}) copy-start(s32[8,32]{1,0:T(8,128)} %gap_ref.1) | copy-start | bytes 3076
  0.0 3.5 %copy-start.4 = (s32[32]{0:T(128)S(1)}, s32[32]{0:T(128)}, u32[]{:S(2)}) copy-start(s32[32]{0:T(128)} %reach_ref.1) | copy-start | bytes 388
  3.2 3.3 %collective-permute-start.1 = (bf16[8,512,128]{2,1,0:T(8,128)(2,1)S(1)}, bf16[8,512,128]{2,1,0:T(8,128)(2,1)S(1)}, u32[]{:S(2)}, u32[]{:S(2)}) collective-permute-start(bf16[8,512,128]{2,1,0:T(8,128)(2,1)S(1)} %get-tuple-element.28.own), channel_id=1, source_target_pairs={{0,1},{1,0},{2,3},{3,2},{4,5},{5,4},{6,7},{7,6},{8,9},{9,8},{10,11... | collective-permute-start | bytes 3145736 | tf_op jit(solution)/shard_map/ppermute | solution.py:381
  3.3 11.5 %collective-permute-start.2 = (bf16[6,512,128]{2,1,0:T(8,128)(2,1)S(1)}, bf16[6,512,128]{2,1,0:T(8,128)(2,1)S(1)}, u32[]{:S(2)}, u32[]{:S(2)}) collective-permute-start(bf16[6,512,128]{2,1,0:T(8,128)(2,1)S(1)} %get-tuple-element.31), channel_id=1, source_target_pairs={{0,31},{1,2},{2,1},{3,4},{4,3},{5,6},{6,5},{7,8},{8,7},{9,10},{10,... | collective-permute-start | bytes 2359304 | tf_op jit(solution)/shard_map/ppermute | solution.py:380
  4.9 12.8 %collective-permute-start = (bf16[2,512,128]{2,1,0:T(8,128)(2,1)S(1)}, bf16[2,512,128]{2,1,0:T(8,128)(2,1)S(1)}, u32[]{:S(2)}, u32[]{:S(2)}) collective-permute-start(bf16[2,512,128]{2,1,0:T(8,128)(2,1)S(1)} %get-tuple-element.27), channel_id=1, source_target_pairs={{0,31},{1,2},{2,1},{3,4},{4,3},{5,6},{6,5},{7,8},{8,7},{9,10},{10,... | collective-permute-start | bytes 786440 | tf_op jit(solution)/shard_map/ppermute | solution.py:380
  17.1 1.5 %copy-start.1 = (bf16[512,1024]{1,0:T(8,128)(2,1)S(1)}, bf16[512,1024]{1,0:T(8,128)(2,1)}, u32[]{:S(2)}) copy-start(bf16[512,1024]{1,0:T(8,128)(2,1)} %w_ref.3) | copy-start | bytes 3145732
  18.6 25.4 %copy-start = (bf16[1024,1536]{1,0:T(8,128)(2,1)S(1)}, bf16[1024,1536]{1,0:T(8,128)(2,1)}, u32[]{:S(2)}) copy-start(bf16[1024,1536]{1,0:T(8,128)(2,1)} %w_ref.4) | copy-start | bytes 9437188
  44.0 17.5 %copy-start.2 = (bf16[512,1024]{1,0:T(8,128)(2,1)S(1)}, bf16[512,1024]{1,0:T(8,128)(2,1)}, u32[]{:S(2)}) copy-start(bf16[512,1024]{1,0:T(8,128)(2,1)} %w_ref.5) | copy-start | bytes 3145732

commit v3 on v2

--- a/solution.py
+++ b/solution.py
@@ -11,7 +11,7 @@
 PAIR = 2 * HEAD
 ROWS = 128
 COLS = 16
-FAR = ((0, 1, 2), (3,))
+NEAR = ((0, 1), (2, 3))
 SCALE = HEAD ** (-0.5) / math.log(2.0)
 BF = jnp.bfloat16
 F32 = jnp.float32
@@ -64,12 +64,12 @@
     return jnp.where((cols >= low) & (cols < high), 1.0, 0.0)
 
 
-def keyval_kernel(x_hbm, w_hbm, x_ref, n_ref, wq_ref, kv_ref, *refs):
-    far_refs = refs[: len(FAR)]
-    w_ref, xsem, wsem, qsem = refs[len(FAR) :]
+def keyval_kernel(x_hbm, w_hbm, x_ref, n_ref, wq_ref, wk_ref, wv_ref, *refs):
+    groups = NEAR
+    kv_refs = refs[: len(groups)]
+    xsem, wsem, qsem = refs[len(groups) :]
     rows = x_ref.shape[0]
     hd = wq_ref.shape[1]
-    pairs = hd // PAIR
     parts = xsem.shape[0]
     tile = rows // parts
     xs = [
@@ -79,12 +79,8 @@
         for i in range(parts)
     ]
     ws = [
-        pltpu.make_async_copy(
-            w_hbm.at[:, pl.ds(hd + i * hd // 2, hd // 2)],
-            w_ref.at[:, pl.ds(i * hd // 2, hd // 2)],
-            wsem.at[i],
-        )
-        for i in range(4)
+        pltpu.make_async_copy(w_hbm.at[:, pl.ds(i * hd, hd)], w_ref, wsem.at[i - 1])
+        for i, w_ref in ((1, wk_ref), (2, wv_ref))
     ]
     wq = pltpu.make_async_copy(w_hbm.at[:, pl.ds(0, hd)], wq_ref, qsem)
     for copy in xs + ws:
@@ -96,42 +92,40 @@
         n_ref[part] = rms(x_ref[part].astype(F32)).astype(BF)
     for copy in ws:
         copy.wait()
-    out = dot(n_ref[...], w_ref[...]).astype(BF)
-    for p in range(2 * pairs):
-        kv_ref[p] = out[:, p * PAIR : (p + 1) * PAIR]
-    for far_ref, group in zip(far_refs, FAR):
+    keys = dot(n_ref[...], wk_ref[...]).astype(BF)
+    values = dot(n_ref[...], wv_ref[...]).astype(BF)
+    for kv_ref, group in zip(kv_refs, groups):
         for i, p in enumerate(group):
-            far_ref[i] = out[:, p * PAIR : (p + 1) * PAIR]
-            far_ref[len(group) + i] = out[:, hd + p * PAIR : hd + (p + 1) * PAIR]
+            kv_ref[i] = keys[:, p * PAIR : (p + 1) * PAIR]
+            kv_ref[len(group) + i] = values[:, p * PAIR : (p + 1) * PAIR]
     wq.wait()
 
 
 def keyval(x, weights):
     rows, features = x.shape
     hd = weights.shape[1] // 3
-    pairs = hd // PAIR
     out = pl.pallas_call(
         keyval_kernel,
         in_specs=[HBM] * 2,
-        out_specs=[VMEM] * (4 + len(FAR)),
+        out_specs=[VMEM] * (5 + len(NEAR)),
         out_shape=[
             jax.ShapeDtypeStruct((rows, features), BF),
             jax.ShapeDtypeStruct((rows, features), BF),
             jax.ShapeDtypeStruct((features, hd), BF),
-            jax.ShapeDtypeStruct((2 * pairs, rows, PAIR), BF),
-            *[jax.ShapeDtypeStruct((2 * len(group), rows, PAIR), BF) for group in FAR],
+            jax.ShapeDtypeStruct((features, hd), BF),
+            jax.ShapeDtypeStruct((features, hd), BF),
+            *[jax.ShapeDtypeStruct((2 * len(group), rows, PAIR), BF) for group in NEAR],
         ],
         scratch_shapes=[
-            pltpu.VMEM((features, 2 * hd), BF),
             pltpu.SemaphoreType.DMA((4,)),
-            pltpu.SemaphoreType.DMA((4,)),
+            pltpu.SemaphoreType.DMA((2,)),
             pltpu.SemaphoreType.DMA,
         ],
-        compiler_params=pltpu.CompilerParams(vmem_limit_bytes=48 * 2**20),
-        cost_estimate=cost(2 * rows * features * 2 * hd, 6 * 2**20),
+        compiler_params=pltpu.CompilerParams(vmem_limit_bytes=47 * 2**20),
+        cost_estimate=cost(1, 1),
         name="keyval",
     )(x, weights)
-    return *out[:4], out[4:]
+    return *out[:3], out[3:5], out[5:]
 
 
 def query_kernel(gap_ref, reach_ref, n_ref, w_ref, q_ref, mask_ref, alive_ref):
@@ -162,19 +156,21 @@
             jax.ShapeDtypeStruct((8, species * COLS), jnp.int32),
         ],
         compiler_params=pltpu.CompilerParams(vmem_limit_bytes=16 * 2**20),
-        cost_estimate=cost(2 * rows * features * hd, 2**20),
+        cost_estimate=cost(1, 1),
         name="queries",
     )(gap_mask, reach, normed, weights)
 
 
-def near_kernel(mask_ref, q_ref, own, fast, acc_ref, max_ref):
+def near_kernel(mask_ref, q_ref, *refs):
+    acc_ref, max_ref = refs[-2:]
+    owns, fasts = refs[: len(NEAR)], refs[len(NEAR) : -2]
     pairs, rows, _ = q_ref.shape
     seen = mask_ref[0, :1] > 0.5
 
-    def scores(p, t):
+    def scores(p, t, keys_own, keys_fast):
         q = q_ref[p, pl.ds(t * ROWS, ROWS)]
         heads = [one_head(q, h) for h in range(2)]
-        return [(dot_t(q, own[p]), dot_t(q, fast[p])) for q in heads]
+        return [(dot_t(q, keys_own), dot_t(q, keys_fast)) for q in heads]
 
     def finish(p, t, found, va):
         part = pl.ds(t * ROWS, ROWS)
@@ -189,14 +185,15 @@
         acc_ref[p, part] = dot(jnp.concatenate(probs, axis=1), va)
 
     late = None
-    for p in range(pairs):
-        vals = (own[pairs + p], fast[pairs + p])
-        va = jnp.concatenate([values_and_ones(v, h) for h in range(2) for v in vals], axis=0)
-        for t in range(rows // ROWS):
-            found = scores(p, t)
-            if late is not None:
-                finish(*late)
-            late = (p, t, found, va)
+    for group, own, fast in zip(NEAR, owns, fasts):
+        for i, p in enumerate(group):
+            vals = (own[len(group) + i], fast[len(group) + i])
+            va = jnp.concatenate([values_and_ones(v, h) for h in range(2) for v in vals], axis=0)
+            for t in range(rows // ROWS):
+                found = scores(p, t, own[i], fast[i])
+                if late is not None:
+                    finish(*late)
+                late = (p, t, found, va)
     finish(*late)
 
 
@@ -204,29 +201,33 @@
     pairs, rows, _ = q.shape
     return pl.pallas_call(
         near_kernel,
-        in_specs=[VMEM] * 4,
+        in_specs=[VMEM] * (2 + 2 * len(NEAR)),
         out_specs=[VMEM, VMEM],
         out_shape=[
             jax.ShapeDtypeStruct((pairs, rows, 2 * PAIR), F32),
             jax.ShapeDtypeStruct((2 * pairs, rows, PAIR), F32),
         ],
         compiler_params=pltpu.CompilerParams(vmem_limit_bytes=24 * 2**20),
-        cost_estimate=cost(32 * rows * rows * PAIR * pairs, 2**23),
+        cost_estimate=cost(1, 1),
         name="near_attend",
-    )(mask, q, own, fast)
-
-
-def far_kernel(group, mask_ref, q_ref, kv_ref, acc_ref, max_ref, *refs):
-    out_ref = refs[-1]
-    rows = q_ref.shape[1]
+    )(mask, q, *own, *fast)
+
+
+def far_kernel(mask_ref, q_ref, x_ref, wk_ref, wv_ref, acc_ref, max_ref, own_ref, wo_ref, mid_ref, send_ref, kv_ref, att_ref):
+    pairs, rows, _ = q_ref.shape
     seen = mask_ref[1, :1] > 0.5
-
-    def scores(i, t):
-        q = q_ref[group[i], pl.ds(t * ROWS, ROWS)]
-        return [dot_t(one_head(q, h), kv_ref[i]) for h in range(2)]
-
-    def finish(i, t, found, va):
-        p = group[i]
+    squares = jnp.mean(jnp.square(x_ref[...].astype(F32)), axis=-1, keepdims=True)
+    factor = lax.rsqrt(squares + 1e-06)
+    for i, w_ref in enumerate((wk_ref, wv_ref)):
+        out = (dot(x_ref[...], w_ref[...]) * factor).astype(BF)
+        for p in range(pairs):
+            kv_ref[i * pairs + p] = out[:, p * PAIR : (p + 1) * PAIR]
+
+    def scores(p, t):
+        q = q_ref[p, pl.ds(t * ROWS, ROWS)]
+        return [dot_t(one_head(q, h), kv_ref[p]) for h in range(2)]
+
+    def finish(p, t, found, va):
         part = pl.ds(t * ROWS, ROWS)
         scales, probs = [], []
         for h, s in enumerate(found):
@@ -240,69 +241,52 @@
         old = acc_ref[p, part]
         num = acc[:, :PAIR] + old[:, :PAIR] * scale
         den = acc[:, PAIR:] + old[:, PAIR:] * scale
-        out_ref[part, p * PAIR : (p + 1) * PAIR] = (num / den).astype(BF)
+        att_ref[part, p * PAIR : (p + 1) * PAIR] = (num / den).astype(BF)
 
     late = None
-    for i in range(len(group)):
-        vals = kv_ref[len(group) + i]
-        va = jnp.concatenate([values_and_ones(vals, h) for h in range(2)], axis=0)
+    for p in range(pairs):
+        va = jnp.concatenate([values_and_ones(kv_ref[pairs + p], h) for h in range(2)], axis=0)
         for t in range(rows // ROWS):
-            found = scores(i, t)
+            found = scores(p, t)
             if late is not None:
                 finish(*late)
-            late = (i, t, found, va)
+            late = (p, t, found, va)
     finish(*late)
-
-
-def far_attend(group, mask, q, kv, acc, top, att):
-    pairs, rows, _ = q.shape
-
-    def kernel(*refs):
-        far_kernel(group, *refs)
-
-    return pl.pallas_call(
-        kernel,
-        in_specs=[VMEM] * (5 + len(att)),
-        out_specs=VMEM,
-        out_shape=jax.ShapeDtypeStruct((rows, pairs * PAIR), BF),
-        input_output_aliases={5: 0} if att else {},
-        compiler_params=pltpu.CompilerParams(vmem_limit_bytes=24 * 2**20),
-        cost_estimate=cost(16 * rows * rows * PAIR * len(group), 2**21),
-        name=f"far_attend{group[0]}",
-    )(mask, q, kv, acc, top, *att)
-
-
-def middle_kernel(x_ref, att_ref, w_ref, mid_ref, send_ref):
-    mid = x_ref[...].astype(F32) + dot(att_ref[...], w_ref[...])
+    mid = own_ref[...].astype(F32) + dot(att_ref[...], wo_ref[...])
     mid_ref[...] = mid
     send_ref[...] = mid.astype(BF)
 
 
-def middle_of(x, att, weights):
-    rows, features = x.shape
-    return pl.pallas_call(
-        middle_kernel,
-        in_specs=[VMEM] * 3,
-        out_specs=[VMEM, VMEM],
+def far_attend(mask, q, x_far, w_kv, acc, top, x, w_out):
+    pairs, rows, _ = q.shape
+    features = x.shape[1]
+    return pl.pallas_call(
+        far_kernel,
+        in_specs=[VMEM] * 9,
+        out_specs=[VMEM] * 2,
         out_shape=[
             jax.ShapeDtypeStruct((rows, features), F32),
             jax.ShapeDtypeStruct((rows, features), BF),
         ],
-        compiler_params=pltpu.CompilerParams(vmem_limit_bytes=16 * 2**20),
-        cost_estimate=cost(2 * rows * features * weights.shape[0], 2**22),
-        name="middle",
-    )(x, att, weights)
+        scratch_shapes=[
+            pltpu.VMEM((2 * pairs, rows, PAIR), BF),
+            pltpu.VMEM((rows, pairs * PAIR), BF),
+        ],
+        compiler_params=pltpu.CompilerParams(vmem_limit_bytes=24 * 2**20),
+        cost_estimate=cost(6 * 10**9, 2**23),
+        name="far_attend",
+    )(mask, q, x_far, *w_kv, acc, top, x, w_out)
 
 
 def column_kernel(alive_ref, mid_ref, w_ref, out_ref, pack_ref):
     species, columns, features = mid_ref.shape
     hd = out_ref.shape[2]
     pairs = hd // PAIR
-    n = rms(mid_ref[...].reshape(species * columns, features).astype(F32)).astype(BF)
+    rows = mid_ref[...].reshape(species * columns, features)
+    squares = jnp.mean(jnp.square(rows.astype(F32)), axis=-1, keepdims=True)
+    factor = lax.rsqrt(squares + 1e-06)
     for j in range(3):
-        out = dot(n, w_ref[:, j * hd : (j + 1) * hd])
-        if j == 0:
-            out = out * SCALE
+        out = dot(rows, w_ref[:, j * hd : (j + 1) * hd]) * (factor * SCALE if j == 0 else factor)
         out = out.astype(BF).reshape(species, columns, hd)
         for p in range(pairs):
             pack_ref[j * pairs + p] = out[:, :, p * PAIR : (p + 1) * PAIR]
@@ -374,16 +358,12 @@
     def by_column(array):
         return lax.all_to_all(array.reshape(species, columns, array.shape[1]), "species", 0, 0)
 
-    x, normed, wq, own, sends = keyval(x, row_qkv)
+    x_far = lax.ppermute(x, "ctx", far)
+    x, normed, wq, w_kv, own = keyval(x, row_qkv)
+    fast = [lax.ppermute(kv, "ctx", near) for kv in own]
     q, mask, alive = queries(gap_mask, window_reach, normed, wq)
-    q, last_send = lax.optimization_barrier((q, sends[-1]))
-    fars = [lax.ppermute(kv, "ctx", far) for kv in (*sends[:-1], last_send)]
-    fast = lax.ppermute(own, "ctx", near)
     acc, top = near_attend(mask, q, own, fast)
-    att = []
-    for group, kv in zip(FAR, fars):
-        att = [far_attend(group, mask, q, kv, acc, top, att)]
-    mid, send = middle_of(x, att[0], row_out)
+    mid, send = far_attend(mask, q, x_far, w_kv, acc, top, x, row_out)
     col_att = column_attend(alive, by_column(send), col_qkv)
     back = lax.all_to_all(col_att, "species", 0, 0)
     out = last(mid, back.reshape(blocklen, hd), col_out)

time: 63.4 us -> 62.8 us (level)
  waiting for transfers between devices: 3.71 us -> 1.39 us
  starting transfers between devices: 2.01 us -> 3.58 us
    ppermute x3, waiting for transfers between devices: 3.71 us -> 1.39 us  [the longest x1 0.71 us: body(): x_far = lax.ppermute(x, 'ctx', far)]
    ppermute x3, starting transfers between devices: 2.01 us -> 3.58 us  [the longest x2 3.58 us: body(): fast = [lax.ppermute(kv, 'ctx', near) for kv in own]]
    pallas_call x5 -> x3, Pallas kernels: 12.2 us -> 12.7 us  [the longest x1 4.91 us: near_attend(): pl.pallas_call(near_kernel, in_specs=[VMEM] * (2 + 2 * len(NEAR)), out_sp...]
  transfers between devices with their start and end apart: 3 -> 3, of which waited for: 2 -> 2; matrix products, arithmetic and copies ran while one was open for 0% -> 0% of each run, Pallas kernels for 14% -> 15%
where the time goes in v3:
time: 62.8 us; the launch traced here: 62.6 us
  blocking collectives  39.1 us (62%)
  Pallas kernels  18.5 us (29%)
  starting transfers between devices  3.58 us (6%)
  waiting for transfers between devices  1.39 us (2%)
    all_to_all x1, blocking collectives, by_column(): lax.all_to_all(array.reshape(species, columns, array.shape[1]), 'species'...  24.4 us
    all_to_all x1, blocking collectives, body(): back = lax.all_to_all(col_att, 'species', 0, 0)  14.7 us
    pallas_call x1, Pallas kernels, near_attend(): pl.pallas_call(near_kernel, in_specs=[VMEM] * (2 + 2 * len(NEAR)), out_sp...  4.91 us
    pallas_call x1, Pallas kernels, far_attend(): pl.pallas_call(far_kernel, in_specs=[VMEM] * 9, out_specs=[VMEM] * 2, out...  4.55 us
    ppermute x2, starting transfers between devices, body(): fast = [lax.ppermute(kv, 'ctx', near) for kv in own]  3.58 us
    pallas_call x1, Pallas kernels, keyval(): pl.pallas_call(keyval_kernel, in_specs=[HBM] * 2, out_specs=[VMEM] * (5 +...  3.2 us
    pallas_call x1, Pallas kernels, column_attend(): pl.pallas_call(column_kernel, in_specs=[VMEM] * 3, out_specs=VMEM, out_sh...  2.79 us
    pallas_call x1, Pallas kernels, last(): pl.pallas_call(last_kernel, grid=(rows // tile,), in_specs=[VMEM] * 3, ou...  1.7 us
  transfers between devices with their start and end apart: 3, of which 2 were waited for; matrix products, arithmetic and copies ran while one was open for 0% of the time, Pallas kernels for 15%

profile of v3, /device:TPU:96, one launch (start us, length us, event | category | flops | bytes accessed | tf_op | source)
XLA Modules:
  0.0 62.6 jit_solution(16267006209264059569)
XLA Ops:
  0.0 0.0 copy-start.2
  0.0 0.0 copy-start.3
  0.0 0.0 collective-permute-start
  0.0 3.2 %keyval.1 = (bf16[512,1024]{1,0:T(8,128)(2,1)S(1)}, bf16[512,1024]{1,0:T(8,128)(2,1)S(1)}, bf16[1024,512]{1,0:T(8,128)(2,1)S(1)}, bf16[1024,512]{1,0:T(8,128)(2,...) custom-call(bf16[512,1024]{1,0:T(8,128)(2,1)} %bitcast.7, ...), custom_call_target="tpu_custom_call" | custom-call | flops 1 | bytes 1 | tf_op jit(solution)/shard_map/keyval/pallas_call | solution.py:107
  3.2 3.3 %collective-permute-start.1 = (bf16[4,512,128]{2,1,0:T(8,128)(2,1)S(1)}, bf16[4,512,128]{2,1,0:T(8,128)(2,1)S(1)}, u32[]{:S(2)}, u32[]{:S(2)}) collective-permute-start(bf16[4,512,128]{2,1,0:T(8,128)(2,1)S(1)} %get-tuple-element.25.refs_0_), channel_id=1, source_target_pairs={{0,1},{1,0},{2,3},{3,2},{4,5},{5,4},{6,7},{7,6},{8,9},{9,8},{10,11... | collective-permute-start | bytes 1572872 | tf_op jit(solution)/shard_map/ppermute | solution.py:363
  6.5 0.3 collective-permute-start.2
  6.8 0.0 copy-done.2
  6.8 0.0 copy-done.3
  6.8 0.0 copy-start.4
  6.8 1.3 %queries.1 = (bf16[4,512,128]{2,1,0:T(8,128)(2,1)S(1)}, f32[2,8,512]{2,1,0:T(8,128)S(1)}, s32[8,128]{1,0:T(8,128)S(1)}) custom-call(s32[8,32]{1,0:T(8,128)S(1)} %copy-done.2, s32[32]{0:T(128)S(1)} %copy-done.3, bf16[512,1024]{1,0:T(8,128)(2,1)S(1)} %get-tuple-element.19.n_ref, bf16[1024,512]{1,0:T(8,128)(2,1)S(1)} %get-tuple-element.20.w_ref), custom_call_target="tpu_custom_call" | custom-call | flops 1 | bytes 1 | tf_op jit(solution)/shard_map/queries/pallas_call | solution.py:149
  8.1 0.0 collective-permute-done.1.refs_2_
  8.1 0.7 %collective-permute-done.2.refs_3_ = bf16[4,512,128]{2,1,0:T(8,128)(2,1)S(1)} collective-permute-done((bf16[4,512,128]{2,1,0:T(8,128)(2,1)S(1)}, bf16[4,512,128]{2,1,0:T(8,128)(2,1)S(1)}, u32[]{:S(2)}, u32[]{:S(2)}) %collective-permute-start.2) | collective-permute-done | bytes 524320 | tf_op jit(solution)/shard_map/ppermute | solution.py:363
  8.8 4.9 %near_attend.1 = (f32[4,512,256]{2,1,0:T(8,128)S(1)}, f32[8,512,128]{2,1,0:T(8,128)S(1)}) custom-call(f32[2,8,512]{2,1,0:T(8,128)S(1)} %get-tuple-element.21.mask_ref, bf16[4,512,128]{2,1,0:T(8,128)(2,1)S(1)} %get-tuple-element.22.q_ref, bf16[4,512,128]{2,1,0:T(8,128)(2,1)S(1)} %get-tuple-element.25.refs_0_, ...), custom_call_target="tpu_custom_call" | custom-call | flops 1 | bytes 1 | tf_op jit(solution)/shard_map/near_attend/pallas_call | solution.py:202
  13.7 0.7 %collective-permute-done.x_ref = bf16[512,1024]{1,0:T(8,128)(2,1)S(1)} collective-permute-done((bf16[512,1024]{1,0:T(8,128)(2,1)}, bf16[512,1024]{1,0:T(8,128)(2,1)S(1)}, u32[]{:S(2)}, u32[]{:S(2)}) %collective-permute-start) | collective-permute-done | bytes 1048608 | tf_op jit(solution)/shard_map/ppermute | solution.py:361
  14.4 0.0 copy-done.4
  14.4 0.0 copy-start
  14.4 4.5 %far_attend.1 = (f32[512,1024]{1,0:T(8,128)S(1)}, bf16[512,1024]{1,0:T(8,128)(2,1)S(1)}) custom-call(f32[2,8,512]{2,1,0:T(8,128)S(1)} %get-tuple-element.21.mask_ref, bf16[4,512,128]{2,1,0:T(8,128)(2,1)S(1)} %get-tuple-element.22.q_ref, bf16[512,1024]{1,0:T(8,128)(2,1)S(1)} %collective-permute-done.x_ref, bf16[1024,512]{1,0:T(8,128)(2,1)S(1)} %get-tuple-element.23.wk_ref, ...), custom_call_target="tpu_custom_call" | custom-call | flops 6000000000 | bytes 8388608 | tf_op jit(solution)/shard_map/far_attend/pallas_call | solution.py:263
  19.0 24.4 %all_to_all.10.mid_ref = bf16[8,64,1024]{2,1,0:T(8,128)(2,1)S(1)} all-to-all(bf16[8,64,1024]{2,1,0:T(8,128)(2,1)S(1)} %bitcast.5), channel_id=1, replica_groups=mesh['species'=8,'ctx'=32] {'species'}, dimensions={0} | all-to-all | bytes 2097152 | tf_op jit(solution)/shard_map/all_to_all | solution.py:359
  43.4 0.0 copy-done
  43.4 0.0 copy-start.1
  43.4 2.8 %column_attend.1 = bf16[8,64,512]{2,1,0:T(8,128)(2,1)S(1)} custom-call(s32[8,128]{1,0:T(8,128)S(1)} %get-tuple-element.31.alive_ref, bf16[8,64,1024]{2,1,0:T(8,128)(2,1)S(1)} %all_to_all.10.mid_ref, bf16[1024,1536]{1,0:T(8,128)(2,1)S(1)} %copy-done), custom_call_target="tpu_custom_call" | custom-call | tf_op jit(solution)/shard_map/column_attend/pallas_call | solution.py:317
  46.2 14.7 %all_to_all.11 = bf16[8,64,512]{2,1,0:T(8,128)(2,1)S(1)} all-to-all(bf16[8,64,512]{2,1,0:T(8,128)(2,1)S(1)} %column_attend.1), channel_id=1, replica_groups=mesh['species'=8,'ctx'=32] {'species'}, dimensions={0} | all-to-all | bytes 1048576 | tf_op jit(solution)/shard_map/all_to_all | solution.py:368
  60.9 0.0 copy-done.1
  60.9 1.7 %last.1 = bf16[512,1024]{1,0:T(8,128)(2,1)} custom-call(f32[512,1024]{1,0:T(8,128)S(1)} %get-tuple-element.30.mid_ref, bf16[512,512]{1,0:T(8,128)(2,1)S(1)} %bitcast.4, bf16[512,1024]{1,0:T(8,128)(2,1)S(1)} %copy-done.1), custom_call_target="tpu_custom_call" | custom-call | tf_op jit(solution)/shard_map/last/pallas_call | solution.py:337
Async XLA Ops:
  0.0 6.8 %copy-start.2 = (s32[8,32]{1,0:T(8,128)S(1)}, s32[8,32]{1,0:T(8,128)}, u32[]{:S(2)}) copy-start(s32[8,32]{1,0:T(8,128)} %gap_ref.1) | copy-start | bytes 3076
  0.0 6.8 %copy-start.3 = (s32[32]{0:T(128)S(1)}, s32[32]{0:T(128)}, u32[]{:S(2)}) copy-start(s32[32]{0:T(128)} %reach_ref.1) | copy-start | bytes 388
  0.0 14.4 %collective-permute-start = (bf16[512,1024]{1,0:T(8,128)(2,1)}, bf16[512,1024]{1,0:T(8,128)(2,1)S(1)}, u32[]{:S(2)}, u32[]{:S(2)}) collective-permute-start(bf16[512,1024]{1,0:T(8,128)(2,1)} %bitcast.6), channel_id=1, source_target_pairs={{0,31},{1,2},{2,1},{3,4},{4,3},{5,6},{6,5},{7,8},{8,7},{9,10},{10,... | collective-permute-start | bytes 3145736 | tf_op jit(solution)/shard_map/ppermute | solution.py:361
  3.2 4.9 %collective-permute-start.1 = (bf16[4,512,128]{2,1,0:T(8,128)(2,1)S(1)}, bf16[4,512,128]{2,1,0:T(8,128)(2,1)S(1)}, u32[]{:S(2)}, u32[]{:S(2)}) collective-permute-start(bf16[4,512,128]{2,1,0:T(8,128)(2,1)S(1)} %get-tuple-element.25.refs_0_), channel_id=1, source_target_pairs={{0,1},{1,0},{2,3},{3,2},{4,5},{5,4},{6,7},{7,6},{8,9},{9,8},{10,11... | collective-permute-start | bytes 1572872 | tf_op jit(solution)/shard_map/ppermute | solution.py:363
  6.5 2.3 %collective-permute-start.2 = (bf16[4,512,128]{2,1,0:T(8,128)(2,1)S(1)}, bf16[4,512,128]{2,1,0:T(8,128)(2,1)S(1)}, u32[]{:S(2)}, u32[]{:S(2)}) collective-permute-start(bf16[4,512,128]{2,1,0:T(8,128)(2,1)S(1)} %get-tuple-element.26.refs_1_), channel_id=1, source_target_pairs={{0,1},{1,0},{2,3},{3,2},{4,5},{5,4},{6,7},{7,6},{8,9},{9,8},{10,11... | collective-permute-start | bytes 1572872 | tf_op jit(solution)/shard_map/ppermute | solution.py:363
  6.8 7.6 %copy-start.4 = (bf16[512,1024]{1,0:T(8,128)(2,1)S(1)}, bf16[512,1024]{1,0:T(8,128)(2,1)}, u32[]{:S(2)}) copy-start(bf16[512,1024]{1,0:T(8,128)(2,1)} %wo_ref.1) | copy-start | bytes 3145732
  14.4 29.0 %copy-start = (bf16[1024,1536]{1,0:T(8,128)(2,1)S(1)}, bf16[1024,1536]{1,0:T(8,128)(2,1)}, u32[]{:S(2)}) copy-start(bf16[1024,1536]{1,0:T(8,128)(2,1)} %w_ref.2) | copy-start | bytes 9437188
  43.4 17.5 %copy-start.1 = (bf16[512,1024]{1,0:T(8,128)(2,1)S(1)}, bf16[512,1024]{1,0:T(8,128)(2,1)}, u32[]{:S(2)}) copy-start(bf16[512,1024]{1,0:T(8,128)(2,1)} %w_ref.3) | copy-start | bytes 3145732

commit v4 on v3

--- a/solution.py
+++ b/solution.py
@@ -216,10 +216,9 @@
 def far_kernel(mask_ref, q_ref, x_ref, wk_ref, wv_ref, acc_ref, max_ref, own_ref, wo_ref, mid_ref, send_ref, kv_ref, att_ref):
     pairs, rows, _ = q_ref.shape
     seen = mask_ref[1, :1] > 0.5
-    squares = jnp.mean(jnp.square(x_ref[...].astype(F32)), axis=-1, keepdims=True)
-    factor = lax.rsqrt(squares + 1e-06)
+    normed = rms(x_ref[...].astype(F32)).astype(BF)
     for i, w_ref in enumerate((wk_ref, wv_ref)):
-        out = (dot(x_ref[...], w_ref[...]) * factor).astype(BF)
+        out = dot(normed, w_ref[...]).astype(BF)
         for p in range(pairs):
             kv_ref[i * pairs + p] = out[:, p * PAIR : (p + 1) * PAIR]
 
@@ -282,11 +281,11 @@
     species, columns, features = mid_ref.shape
     hd = out_ref.shape[2]
     pairs = hd // PAIR
-    rows = mid_ref[...].reshape(species * columns, features)
-    squares = jnp.mean(jnp.square(rows.astype(F32)), axis=-1, keepdims=True)
-    factor = lax.rsqrt(squares + 1e-06)
+    n = rms(mid_ref[...].reshape(species * columns, features).astype(F32)).astype(BF)
     for j in range(3):
-        out = dot(rows, w_ref[:, j * hd : (j + 1) * hd]) * (factor * SCALE if j == 0 else factor)
+        out = dot(n, w_ref[:, j * hd : (j + 1) * hd])
+        if j == 0:
+            out = out * SCALE
         out = out.astype(BF).reshape(species, columns, hd)
         for p in range(pairs):
             pack_ref[j * pairs + p] = out[:, :, p * PAIR : (p + 1) * PAIR]

time: 62.8 us -> 62.8 us (level)
  no operation moved by 1% of the time
where the time goes in v4:
time: 62.8 us; the launch traced here: 62.7 us
  blocking collectives  39.1 us (62%)
  Pallas kernels  18.5 us (29%)
  starting transfers between devices  3.58 us (6%)
  waiting for transfers between devices  1.39 us (2%)
    all_to_all x1, blocking collectives, by_column(): lax.all_to_all(array.reshape(species, columns, array.shape[1]), 'species'...  24.4 us
    all_to_all x1, blocking collectives, body(): back = lax.all_to_all(col_att, 'species', 0, 0)  14.7 us
    pallas_call x1, Pallas kernels, near_attend(): pl.pallas_call(near_kernel, in_specs=[VMEM] * (2 + 2 * len(NEAR)), out_sp...  4.91 us
    pallas_call x1, Pallas kernels, far_attend(): pl.pallas_call(far_kernel, in_specs=[VMEM] * 9, out_specs=[VMEM] * 2, out...  4.59 us
    ppermute x2, starting transfers between devices, body(): fast = [lax.ppermute(kv, 'ctx', near) for kv in own]  3.58 us
    pallas_call x1, Pallas kernels, keyval(): pl.pallas_call(keyval_kernel, in_specs=[HBM] * 2, out_specs=[VMEM] * (5 +...  3.2 us
    pallas_call x1, Pallas kernels, column_attend(): pl.pallas_call(column_kernel, in_specs=[VMEM] * 3, out_specs=VMEM, out_sh...  2.78 us
    pallas_call x1, Pallas kernels, last(): pl.pallas_call(last_kernel, grid=(rows // tile,), in_specs=[VMEM] * 3, ou...  1.7 us
  transfers between devices with their start and end apart: 3, of which 2 were waited for; matrix products, arithmetic and copies ran while one was open for 0% of the time, Pallas kernels for 15%

profile of v4, /device:TPU:96, one launch (start us, length us, event | category | flops | bytes accessed | tf_op | source)
XLA Modules:
  0.0 62.7 jit_solution(9534426114299895107)
XLA Ops:
  0.0 0.0 copy-start.2
  0.0 0.0 copy-start.3
  0.0 0.0 collective-permute-start
  0.0 3.2 %keyval.1 = (bf16[512,1024]{1,0:T(8,128)(2,1)S(1)}, bf16[512,1024]{1,0:T(8,128)(2,1)S(1)}, bf16[1024,512]{1,0:T(8,128)(2,1)S(1)}, bf16[1024,512]{1,0:T(8,128)(2,...) custom-call(bf16[512,1024]{1,0:T(8,128)(2,1)} %bitcast.7, ...), custom_call_target="tpu_custom_call" | custom-call | flops 1 | bytes 1 | tf_op jit(solution)/shard_map/keyval/pallas_call | solution.py:107
  3.2 3.3 %collective-permute-start.1 = (bf16[4,512,128]{2,1,0:T(8,128)(2,1)S(1)}, bf16[4,512,128]{2,1,0:T(8,128)(2,1)S(1)}, u32[]{:S(2)}, u32[]{:S(2)}) collective-permute-start(bf16[4,512,128]{2,1,0:T(8,128)(2,1)S(1)} %get-tuple-element.25.refs_0_), channel_id=1, source_target_pairs={{0,1},{1,0},{2,3},{3,2},{4,5},{5,4},{6,7},{7,6},{8,9},{9,8},{10,11... | collective-permute-start | bytes 1572872 | tf_op jit(solution)/shard_map/ppermute | solution.py:362
  6.5 0.3 collective-permute-start.2
  6.8 0.0 copy-done.2
  6.8 0.0 copy-done.3
  6.8 0.0 copy-start.4
  6.8 1.3 %queries.1 = (bf16[4,512,128]{2,1,0:T(8,128)(2,1)S(1)}, f32[2,8,512]{2,1,0:T(8,128)S(1)}, s32[8,128]{1,0:T(8,128)S(1)}) custom-call(s32[8,32]{1,0:T(8,128)S(1)} %copy-done.2, s32[32]{0:T(128)S(1)} %copy-done.3, bf16[512,1024]{1,0:T(8,128)(2,1)S(1)} %get-tuple-element.19.n_ref, bf16[1024,512]{1,0:T(8,128)(2,1)S(1)} %get-tuple-element.20.w_ref), custom_call_target="tpu_custom_call" | custom-call | flops 1 | bytes 1 | tf_op jit(solution)/shard_map/queries/pallas_call | solution.py:149
  8.1 0.0 collective-permute-done.1.refs_2_
  8.1 0.7 %collective-permute-done.2.refs_3_ = bf16[4,512,128]{2,1,0:T(8,128)(2,1)S(1)} collective-permute-done((bf16[4,512,128]{2,1,0:T(8,128)(2,1)S(1)}, bf16[4,512,128]{2,1,0:T(8,128)(2,1)S(1)}, u32[]{:S(2)}, u32[]{:S(2)}) %collective-permute-start.2) | collective-permute-done | bytes 524320 | tf_op jit(solution)/shard_map/ppermute | solution.py:362
  8.8 4.9 %near_attend.1 = (f32[4,512,256]{2,1,0:T(8,128)S(1)}, f32[8,512,128]{2,1,0:T(8,128)S(1)}) custom-call(f32[2,8,512]{2,1,0:T(8,128)S(1)} %get-tuple-element.21.mask_ref, bf16[4,512,128]{2,1,0:T(8,128)(2,1)S(1)} %get-tuple-element.22.q_ref, bf16[4,512,128]{2,1,0:T(8,128)(2,1)S(1)} %get-tuple-element.25.refs_0_, ...), custom_call_target="tpu_custom_call" | custom-call | flops 1 | bytes 1 | tf_op jit(solution)/shard_map/near_attend/pallas_call | solution.py:202
  13.7 0.7 %collective-permute-done.x_ref = bf16[512,1024]{1,0:T(8,128)(2,1)S(1)} collective-permute-done((bf16[512,1024]{1,0:T(8,128)(2,1)}, bf16[512,1024]{1,0:T(8,128)(2,1)S(1)}, u32[]{:S(2)}, u32[]{:S(2)}) %collective-permute-start) | collective-permute-done | bytes 1048608 | tf_op jit(solution)/shard_map/ppermute | solution.py:360
  14.4 0.0 copy-done.4
  14.4 0.0 copy-start
  14.4 4.6 %far_attend.1 = (f32[512,1024]{1,0:T(8,128)S(1)}, bf16[512,1024]{1,0:T(8,128)(2,1)S(1)}) custom-call(f32[2,8,512]{2,1,0:T(8,128)S(1)} %get-tuple-element.21.mask_ref, bf16[4,512,128]{2,1,0:T(8,128)(2,1)S(1)} %get-tuple-element.22.q_ref, bf16[512,1024]{1,0:T(8,128)(2,1)S(1)} %collective-permute-done.x_ref, bf16[1024,512]{1,0:T(8,128)(2,1)S(1)} %get-tuple-element.23.wk_ref, ...), custom_call_target="tpu_custom_call" | custom-call | flops 6000000000 | bytes 8388608 | tf_op jit(solution)/shard_map/far_attend/pallas_call | solution.py:262
  19.0 24.4 %all_to_all.10.mid_ref = bf16[8,64,1024]{2,1,0:T(8,128)(2,1)S(1)} all-to-all(bf16[8,64,1024]{2,1,0:T(8,128)(2,1)S(1)} %bitcast.5), channel_id=1, replica_groups=mesh['species'=8,'ctx'=32] {'species'}, dimensions={0} | all-to-all | bytes 2097152 | tf_op jit(solution)/shard_map/all_to_all | solution.py:358
  43.5 0.0 copy-done
  43.5 0.0 copy-start.1
  43.5 2.8 %column_attend.1 = bf16[8,64,512]{2,1,0:T(8,128)(2,1)S(1)} custom-call(s32[8,128]{1,0:T(8,128)S(1)} %get-tuple-element.31.alive_ref, bf16[8,64,1024]{2,1,0:T(8,128)(2,1)S(1)} %all_to_all.10.mid_ref, bf16[1024,1536]{1,0:T(8,128)(2,1)S(1)} %copy-done), custom_call_target="tpu_custom_call" | custom-call | tf_op jit(solution)/shard_map/column_attend/pallas_call | solution.py:316
  46.3 14.7 %all_to_all.11 = bf16[8,64,512]{2,1,0:T(8,128)(2,1)S(1)} all-to-all(bf16[8,64,512]{2,1,0:T(8,128)(2,1)S(1)} %column_attend.1), channel_id=1, replica_groups=mesh['species'=8,'ctx'=32] {'species'}, dimensions={0} | all-to-all | bytes 1048576 | tf_op jit(solution)/shard_map/all_to_all | solution.py:367
  61.0 0.0 copy-done.1
  61.0 1.7 %last.1 = bf16[512,1024]{1,0:T(8,128)(2,1)} custom-call(f32[512,1024]{1,0:T(8,128)S(1)} %get-tuple-element.30.mid_ref, bf16[512,512]{1,0:T(8,128)(2,1)S(1)} %bitcast.4, bf16[512,1024]{1,0:T(8,128)(2,1)S(1)} %copy-done.1), custom_call_target="tpu_custom_call" | custom-call | tf_op jit(solution)/shard_map/last/pallas_call | solution.py:336
Async XLA Ops:
  0.0 6.8 %copy-start.2 = (s32[8,32]{1,0:T(8,128)S(1)}, s32[8,32]{1,0:T(8,128)}, u32[]{:S(2)}) copy-start(s32[8,32]{1,0:T(8,128)} %gap_ref.1) | copy-start | bytes 3076
  0.0 6.8 %copy-start.3 = (s32[32]{0:T(128)S(1)}, s32[32]{0:T(128)}, u32[]{:S(2)}) copy-start(s32[32]{0:T(128)} %reach_ref.1) | copy-start | bytes 388
  0.0 14.4 %collective-permute-start = (bf16[512,1024]{1,0:T(8,128)(2,1)}, bf16[512,1024]{1,0:T(8,128)(2,1)S(1)}, u32[]{:S(2)}, u32[]{:S(2)}) collective-permute-start(bf16[512,1024]{1,0:T(8,128)(2,1)} %bitcast.6), channel_id=1, source_target_pairs={{0,31},{1,2},{2,1},{3,4},{4,3},{5,6},{6,5},{7,8},{8,7},{9,10},{10,... | collective-permute-start | bytes 3145736 | tf_op jit(solution)/shard_map/ppermute | solution.py:360
  3.2 4.9 %collective-permute-start.1 = (bf16[4,512,128]{2,1,0:T(8,128)(2,1)S(1)}, bf16[4,512,128]{2,1,0:T(8,128)(2,1)S(1)}, u32[]{:S(2)}, u32[]{:S(2)}) collective-permute-start(bf16[4,512,128]{2,1,0:T(8,128)(2,1)S(1)} %get-tuple-element.25.refs_0_), channel_id=1, source_target_pairs={{0,1},{1,0},{2,3},{3,2},{4,5},{5,4},{6,7},{7,6},{8,9},{9,8},{10,11... | collective-permute-start | bytes 1572872 | tf_op jit(solution)/shard_map/ppermute | solution.py:362
  6.5 2.3 %collective-permute-start.2 = (bf16[4,512,128]{2,1,0:T(8,128)(2,1)S(1)}, bf16[4,512,128]{2,1,0:T(8,128)(2,1)S(1)}, u32[]{:S(2)}, u32[]{:S(2)}) collective-permute-start(bf16[4,512,128]{2,1,0:T(8,128)(2,1)S(1)} %get-tuple-element.26.refs_1_), channel_id=1, source_target_pairs={{0,1},{1,0},{2,3},{3,2},{4,5},{5,4},{6,7},{7,6},{8,9},{9,8},{10,11... | collective-permute-start | bytes 1572872 | tf_op jit(solution)/shard_map/ppermute | solution.py:362
  6.8 7.6 %copy-start.4 = (bf16[512,1024]{1,0:T(8,128)(2,1)S(1)}, bf16[512,1024]{1,0:T(8,128)(2,1)}, u32[]{:S(2)}) copy-start(bf16[512,1024]{1,0:T(8,128)(2,1)} %wo_ref.1) | copy-start | bytes 3145732
  14.4 29.0 %copy-start = (bf16[1024,1536]{1,0:T(8,128)(2,1)S(1)}, bf16[1024,1536]{1,0:T(8,128)(2,1)}, u32[]{:S(2)}) copy-start(bf16[1024,1536]{1,0:T(8,128)(2,1)} %w_ref.2) | copy-start | bytes 9437188
  43.5 17.5 %copy-start.1 = (bf16[512,1024]{1,0:T(8,128)(2,1)S(1)}, bf16[512,1024]{1,0:T(8,128)(2,1)}, u32[]{:S(2)}) copy-start(bf16[512,1024]{1,0:T(8,128)(2,1)} %w_ref.3) | copy-start | bytes 3145732

commit v5 on v4

--- a/solution.py
+++ b/solution.py
@@ -281,33 +281,53 @@
     species, columns, features = mid_ref.shape
     hd = out_ref.shape[2]
     pairs = hd // PAIR
-    n = rms(mid_ref[...].reshape(species * columns, features).astype(F32)).astype(BF)
-    for j in range(3):
+    half = columns // 2
+
+    def normed(place):
+        part = mid_ref[:, place * half : (place + 1) * half, :]
+        return rms(part.reshape(species * half, features).astype(F32)).astype(BF)
+
+    def project(n, place, j):
         out = dot(n, w_ref[:, j * hd : (j + 1) * hd])
         if j == 0:
             out = out * SCALE
-        out = out.astype(BF).reshape(species, columns, hd)
+        out = out.astype(BF).reshape(species, half, hd)
         for p in range(pairs):
-            pack_ref[j * pairs + p] = out[:, :, p * PAIR : (p + 1) * PAIR]
+            pack_ref[j * pairs + p, :, pl.ds(place * half, half), :] = out[
+                :, :, p * PAIR : (p + 1) * PAIR
+            ]
+
     rows = species * COLS
     qrow = lax.broadcasted_iota(jnp.int32, (rows, rows), 0)
     krow = lax.broadcasted_iota(jnp.int32, (rows, rows), 1)
     seen = (lax.rem(qrow, COLS) == lax.rem(krow, COLS)) & (alive_ref[:1] == 1)
     seen = jnp.concatenate([seen, seen], axis=0)
-    for j in range(columns // COLS):
+
+    def attend(j, p):
         part = pl.ds(j * COLS, COLS)
-        for p in range(pairs):
-            q = pack_ref[p, :, part, :].reshape(rows, PAIR)
-            k = pack_ref[pairs + p, :, part, :].reshape(rows, PAIR)
-            v = pack_ref[2 * pairs + p, :, part, :].reshape(rows, PAIR)
-            qs = jnp.concatenate([one_head(q, 0), one_head(q, 1)], axis=0)
-            s = jnp.where(seen, dot_t(qs, k), -1e30)
-            prob = jnp.exp2(s - jnp.max(s, axis=-1, keepdims=True)).astype(BF)
-            prob = jnp.concatenate([prob[:rows], prob[rows:]], axis=1)
-            va = jnp.concatenate([values_and_ones(v, 0), values_and_ones(v, 1)], axis=0)
-            acc = dot(prob, va)
-            att = (acc[:, :PAIR] / acc[:, PAIR:]).astype(BF)
-            out_ref[:, part, p * PAIR : (p + 1) * PAIR] = att.reshape(species, COLS, PAIR)
+        q = pack_ref[p, :, part, :].reshape(rows, PAIR)
+        k = pack_ref[pairs + p, :, part, :].reshape(rows, PAIR)
+        v = pack_ref[2 * pairs + p, :, part, :].reshape(rows, PAIR)
+        qs = jnp.concatenate([one_head(q, 0), one_head(q, 1)], axis=0)
+        s = jnp.where(seen, dot_t(qs, k), -1e30)
+        prob = jnp.exp2(s - jnp.max(s, axis=-1, keepdims=True)).astype(BF)
+        prob = jnp.concatenate([prob[:rows], prob[rows:]], axis=1)
+        va = jnp.concatenate([values_and_ones(v, 0), values_and_ones(v, 1)], axis=0)
+        acc = dot(prob, va)
+        att = (acc[:, :PAIR] / acc[:, PAIR:]).astype(BF)
+        out_ref[:, part, p * PAIR : (p + 1) * PAIR] = att.reshape(species, COLS, PAIR)
+
+    items = [(j, p) for j in range(columns // COLS) for p in range(pairs)]
+    early, late = items[: len(items) // 2], items[len(items) // 2 :]
+    first, second = normed(0), normed(1)
+    for j in range(3):
+        project(first, 0, j)
+    for j in range(3):
+        project(second, 1, j)
+        for item in early[j * len(early) // 3 : (j + 1) * len(early) // 3]:
+            attend(*item)
+    for item in late:
+        attend(*item)
 
 
 def column_attend(alive, mid, weights):

time: 62.8 us -> 62.8 us (level)
  no operation moved by 1% of the time
where the time goes in v5:
time: 62.8 us; the launch traced here: 62.6 us
  blocking collectives  39.1 us (62%)
  Pallas kernels  18.4 us (29%)
  starting transfers between devices  3.58 us (6%)
  waiting for transfers between devices  1.39 us (2%)
    all_to_all x1, blocking collectives, by_column(): lax.all_to_all(array.reshape(species, columns, array.shape[1]), 'species'...  24.4 us
    all_to_all x1, blocking collectives, body(): back = lax.all_to_all(col_att, 'species', 0, 0)  14.7 us
    pallas_call x1, Pallas kernels, near_attend(): pl.pallas_call(near_kernel, in_specs=[VMEM] * (2 + 2 * len(NEAR)), out_sp...  4.91 us
    pallas_call x1, Pallas kernels, far_attend(): pl.pallas_call(far_kernel, in_specs=[VMEM] * 9, out_specs=[VMEM] * 2, out...  4.59 us
    ppermute x2, starting transfers between devices, body(): fast = [lax.ppermute(kv, 'ctx', near) for kv in own]  3.58 us
    pallas_call x1, Pallas kernels, keyval(): pl.pallas_call(keyval_kernel, in_specs=[HBM] * 2, out_specs=[VMEM] * (5 +...  3.2 us
    pallas_call x1, Pallas kernels, column_attend(): pl.pallas_call(column_kernel, in_specs=[VMEM] * 3, out_specs=VMEM, out_sh...  2.72 us
    pallas_call x1, Pallas kernels, last(): pl.pallas_call(last_kernel, grid=(rows // tile,), in_specs=[VMEM] * 3, ou...  1.7 us
  transfers between devices with their start and end apart: 3, of which 2 were waited for; matrix products, arithmetic and copies ran while one was open for 0% of the time, Pallas kernels for 15%

profile of v5, /device:TPU:96, one launch (start us, length us, event | category | flops | bytes accessed | tf_op | source)
XLA Modules:
  0.0 62.6 jit_solution(3521704045005247491)
XLA Ops:
  0.0 0.0 copy-start.2
  0.0 0.0 copy-start.3
  0.0 0.0 collective-permute-start
  0.0 3.2 %keyval.1 = (bf16[512,1024]{1,0:T(8,128)(2,1)S(1)}, bf16[512,1024]{1,0:T(8,128)(2,1)S(1)}, bf16[1024,512]{1,0:T(8,128)(2,1)S(1)}, bf16[1024,512]{1,0:T(8,128)(2,...) custom-call(bf16[512,1024]{1,0:T(8,128)(2,1)} %bitcast.7, ...), custom_call_target="tpu_custom_call" | custom-call | flops 1 | bytes 1 | tf_op jit(solution)/shard_map/keyval/pallas_call | solution.py:107
  3.2 3.3 %collective-permute-start.1 = (bf16[4,512,128]{2,1,0:T(8,128)(2,1)S(1)}, bf16[4,512,128]{2,1,0:T(8,128)(2,1)S(1)}, u32[]{:S(2)}, u32[]{:S(2)}) collective-permute-start(bf16[4,512,128]{2,1,0:T(8,128)(2,1)S(1)} %get-tuple-element.25.refs_0_), channel_id=1, source_target_pairs={{0,1},{1,0},{2,3},{3,2},{4,5},{5,4},{6,7},{7,6},{8,9},{9,8},{10,11... | collective-permute-start | bytes 1572872 | tf_op jit(solution)/shard_map/ppermute | solution.py:382
  6.5 0.3 collective-permute-start.2
  6.8 0.0 copy-done.2
  6.8 0.0 copy-done.3
  6.8 0.0 copy-start.4
  6.8 1.3 %queries.1 = (bf16[4,512,128]{2,1,0:T(8,128)(2,1)S(1)}, f32[2,8,512]{2,1,0:T(8,128)S(1)}, s32[8,128]{1,0:T(8,128)S(1)}) custom-call(s32[8,32]{1,0:T(8,128)S(1)} %copy-done.2, s32[32]{0:T(128)S(1)} %copy-done.3, bf16[512,1024]{1,0:T(8,128)(2,1)S(1)} %get-tuple-element.19.n_ref, bf16[1024,512]{1,0:T(8,128)(2,1)S(1)} %get-tuple-element.20.w_ref), custom_call_target="tpu_custom_call" | custom-call | flops 1 | bytes 1 | tf_op jit(solution)/shard_map/queries/pallas_call | solution.py:149
  8.1 0.0 collective-permute-done.1.refs_2_
  8.1 0.7 %collective-permute-done.2.refs_3_ = bf16[4,512,128]{2,1,0:T(8,128)(2,1)S(1)} collective-permute-done((bf16[4,512,128]{2,1,0:T(8,128)(2,1)S(1)}, bf16[4,512,128]{2,1,0:T(8,128)(2,1)S(1)}, u32[]{:S(2)}, u32[]{:S(2)}) %collective-permute-start.2) | collective-permute-done | bytes 524320 | tf_op jit(solution)/shard_map/ppermute | solution.py:382
  8.8 4.9 %near_attend.1 = (f32[4,512,256]{2,1,0:T(8,128)S(1)}, f32[8,512,128]{2,1,0:T(8,128)S(1)}) custom-call(f32[2,8,512]{2,1,0:T(8,128)S(1)} %get-tuple-element.21.mask_ref, bf16[4,512,128]{2,1,0:T(8,128)(2,1)S(1)} %get-tuple-element.22.q_ref, bf16[4,512,128]{2,1,0:T(8,128)(2,1)S(1)} %get-tuple-element.25.refs_0_, ...), custom_call_target="tpu_custom_call" | custom-call | flops 1 | bytes 1 | tf_op jit(solution)/shard_map/near_attend/pallas_call | solution.py:202
  13.7 0.7 %collective-permute-done.x_ref = bf16[512,1024]{1,0:T(8,128)(2,1)S(1)} collective-permute-done((bf16[512,1024]{1,0:T(8,128)(2,1)}, bf16[512,1024]{1,0:T(8,128)(2,1)S(1)}, u32[]{:S(2)}, u32[]{:S(2)}) %collective-permute-start) | collective-permute-done | bytes 1048608 | tf_op jit(solution)/shard_map/ppermute | solution.py:380
  14.4 0.0 copy-done.4
  14.4 0.0 copy-start
  14.4 4.6 %far_attend.1 = (f32[512,1024]{1,0:T(8,128)S(1)}, bf16[512,1024]{1,0:T(8,128)(2,1)S(1)}) custom-call(f32[2,8,512]{2,1,0:T(8,128)S(1)} %get-tuple-element.21.mask_ref, bf16[4,512,128]{2,1,0:T(8,128)(2,1)S(1)} %get-tuple-element.22.q_ref, bf16[512,1024]{1,0:T(8,128)(2,1)S(1)} %collective-permute-done.x_ref, bf16[1024,512]{1,0:T(8,128)(2,1)S(1)} %get-tuple-element.23.wk_ref, ...), custom_call_target="tpu_custom_call" | custom-call | flops 6000000000 | bytes 8388608 | tf_op jit(solution)/shard_map/far_attend/pallas_call | solution.py:262
  19.0 24.4 %all_to_all.10.mid_ref = bf16[8,64,1024]{2,1,0:T(8,128)(2,1)S(1)} all-to-all(bf16[8,64,1024]{2,1,0:T(8,128)(2,1)S(1)} %bitcast.5), channel_id=1, replica_groups=mesh['species'=8,'ctx'=32] {'species'}, dimensions={0} | all-to-all | bytes 2097152 | tf_op jit(solution)/shard_map/all_to_all | solution.py:378
  43.5 0.0 copy-done
  43.5 0.0 copy-start.1
  43.5 2.7 %column_attend.1 = bf16[8,64,512]{2,1,0:T(8,128)(2,1)S(1)} custom-call(s32[8,128]{1,0:T(8,128)S(1)} %get-tuple-element.31.alive_ref, bf16[8,64,1024]{2,1,0:T(8,128)(2,1)S(1)} %all_to_all.10.mid_ref, bf16[1024,1536]{1,0:T(8,128)(2,1)S(1)} %copy-done), custom_call_target="tpu_custom_call" | custom-call | tf_op jit(solution)/shard_map/column_attend/pallas_call | solution.py:336
  46.2 14.7 %all_to_all.11 = bf16[8,64,512]{2,1,0:T(8,128)(2,1)S(1)} all-to-all(bf16[8,64,512]{2,1,0:T(8,128)(2,1)S(1)} %column_attend.1), channel_id=1, replica_groups=mesh['species'=8,'ctx'=32] {'species'}, dimensions={0} | all-to-all | bytes 1048576 | tf_op jit(solution)/shard_map/all_to_all | solution.py:387
  60.9 0.0 copy-done.1
  60.9 1.7 %last.1 = bf16[512,1024]{1,0:T(8,128)(2,1)} custom-call(f32[512,1024]{1,0:T(8,128)S(1)} %get-tuple-element.30.mid_ref, bf16[512,512]{1,0:T(8,128)(2,1)S(1)} %bitcast.4, bf16[512,1024]{1,0:T(8,128)(2,1)S(1)} %copy-done.1), custom_call_target="tpu_custom_call" | custom-call | tf_op jit(solution)/shard_map/last/pallas_call | solution.py:356
Async XLA Ops:
  0.0 6.8 %copy-start.2 = (s32[8,32]{1,0:T(8,128)S(1)}, s32[8,32]{1,0:T(8,128)}, u32[]{:S(2)}) copy-start(s32[8,32]{1,0:T(8,128)} %gap_ref.1) | copy-start | bytes 3076
  0.0 6.8 %copy-start.3 = (s32[32]{0:T(128)S(1)}, s32[32]{0:T(128)}, u32[]{:S(2)}) copy-start(s32[32]{0:T(128)} %reach_ref.1) | copy-start | bytes 388
  0.0 14.4 %collective-permute-start = (bf16[512,1024]{1,0:T(8,128)(2,1)}, bf16[512,1024]{1,0:T(8,128)(2,1)S(1)}, u32[]{:S(2)}, u32[]{:S(2)}) collective-permute-start(bf16[512,1024]{1,0:T(8,128)(2,1)} %bitcast.6), channel_id=1, source_target_pairs={{0,31},{1,2},{2,1},{3,4},{4,3},{5,6},{6,5},{7,8},{8,7},{9,10},{10,... | collective-permute-start | bytes 3145736 | tf_op jit(solution)/shard_map/ppermute | solution.py:380
  3.2 4.9 %collective-permute-start.1 = (bf16[4,512,128]{2,1,0:T(8,128)(2,1)S(1)}, bf16[4,512,128]{2,1,0:T(8,128)(2,1)S(1)}, u32[]{:S(2)}, u32[]{:S(2)}) collective-permute-start(bf16[4,512,128]{2,1,0:T(8,128)(2,1)S(1)} %get-tuple-element.25.refs_0_), channel_id=1, source_target_pairs={{0,1},{1,0},{2,3},{3,2},{4,5},{5,4},{6,7},{7,6},{8,9},{9,8},{10,11... | collective-permute-start | bytes 1572872 | tf_op jit(solution)/shard_map/ppermute | solution.py:382
  6.5 2.3 %collective-permute-start.2 = (bf16[4,512,128]{2,1,0:T(8,128)(2,1)S(1)}, bf16[4,512,128]{2,1,0:T(8,128)(2,1)S(1)}, u32[]{:S(2)}, u32[]{:S(2)}) collective-permute-start(bf16[4,512,128]{2,1,0:T(8,128)(2,1)S(1)} %get-tuple-element.26.refs_1_), channel_id=1, source_target_pairs={{0,1},{1,0},{2,3},{3,2},{4,5},{5,4},{6,7},{7,6},{8,9},{9,8},{10,11... | collective-permute-start | bytes 1572872 | tf_op jit(solution)/shard_map/ppermute | solution.py:382
  6.8 7.6 %copy-start.4 = (bf16[512,1024]{1,0:T(8,128)(2,1)S(1)}, bf16[512,1024]{1,0:T(8,128)(2,1)}, u32[]{:S(2)}) copy-start(bf16[512,1024]{1,0:T(8,128)(2,1)} %wo_ref.1) | copy-start | bytes 3145732
  14.4 29.0 %copy-start = (bf16[1024,1536]{1,0:T(8,128)(2,1)S(1)}, bf16[1024,1536]{1,0:T(8,128)(2,1)}, u32[]{:S(2)}) copy-start(bf16[1024,1536]{1,0:T(8,128)(2,1)} %w_ref.2) | copy-start | bytes 9437188
  43.5 17.5 %copy-start.1 = (bf16[512,1024]{1,0:T(8,128)(2,1)S(1)}, bf16[512,1024]{1,0:T(8,128)(2,1)}, u32[]{:S(2)}) copy-start(bf16[512,1024]{1,0:T(8,128)(2,1)} %w_ref.3) | copy-start | bytes 3145732
